TPU v7x, 256 devices: a whole 4x4x8 slice. The times are simulated.
256 devices in a mesh: ctx: 16 (over z, x_lo), tp: 8 (over y, core), rep: 2 (over x_hi).
Axes of the slice: x: 4 (x_hi: 2, x_lo: 2; x = x_hi * 2 + x_lo), y: 4, z: 8, core: 2. Of those that a mesh axis runs over, the one named last changes fastest.
Arguments:
- queries: bfloat16 [2048, 8192], P(('rep', 'ctx'), 'tp'), parts along dimension 0, may hold values from -12 to 12
- new_keys: bfloat16 [2048, 1024], P(('rep', 'ctx'), 'tp'), parts along dimension 0, may hold values from -4 to 4
- new_values: bfloat16 [2048, 1024], P(('rep', 'ctx'), 'tp'), parts along dimension 0, may hold values from -4 to 4
- cache_keys: bfloat16 [131072, 1024], P(('rep', 'ctx'), 'tp'), parts along dimension 0, may hold values from -4 to 4
- cache_values: bfloat16 [131072, 1024], P(('rep', 'ctx'), 'tp'), parts along dimension 0, may hold values from -4 to 4
- block_owner: int32 [512], P(('rep', 'ctx')), parts along dimension 0, may hold values from 0 to 255, as said below
- history_len: int32 [4], P('rep'), parts along dimension 0, may hold values from 8192 to 32768, as said below
Outputs:
- attended: float32 [2048, 8192], P(('rep', 'ctx'), 'tp'), parts along dimension 0
There are 2 independent parts, one for each index of `rep`. A program takes and returns all parts, laid end to end along the dimension named above; each array names one. Nothing has to cross between parts.
Inputs may be any that keep to these rules, and one draw needn't show every extreme that they name: block_owner is a permutation of 0 to 255; logical block b of request r lies on ctx index (b + o_r) mod 16 for an offset o_r of the request. `history_len`: one request has a full history.
All inputs are finite; a program needn't handle non-finite values.
Results may differ from a plain program's by a relative error of at most 0.009.
Values may be sent and summed in bfloat16 or wider, within the bound.
A program may use at most 64 MiB of HBM per device.

v0:
```python
import math

import jax
import jax.numpy as jnp
from jax import lax
from jax.sharding import PartitionSpec as P

HD = 128
REQS = 2
BLOCK = 256


def local(queries, new_keys, new_values, cache_keys, cache_values, block_owner, history_len):
    parts = lax.axis_size("ctx")
    me_index = lax.axis_index("ctx")
    here = queries.shape[0]
    kv_local = new_keys.shape[1] // HD
    q_local = queries.shape[1] // HD
    grp = q_local // kv_local
    tok = here * parts // REQS
    blocks = block_owner.shape[0]
    per_req = blocks // REQS
    capacity = blocks * parts // REQS
    scale = 1.0 / math.sqrt(HD)
    key_req = block_owner // capacity
    key_base = block_owner % capacity * BLOCK
    order = jnp.argsort(key_req, stable=True)
    grouped_k = cache_keys.reshape(blocks, BLOCK, kv_local, HD)[order].reshape(
        REQS, per_req, BLOCK, kv_local, HD
    )
    grouped_v = cache_values.reshape(blocks, BLOCK, kv_local, HD)[order].reshape(
        REQS, per_req, BLOCK, kv_local, HD
    )
    grouped_base = key_base[order].reshape(REQS, per_req)
    new_rows = me_index * here + jnp.arange(here, dtype=jnp.int32)
    new_req = new_rows // tok
    new_index = new_rows % tok
    fresh_k = new_keys.reshape(here, kv_local, HD)
    fresh_v = new_values.reshape(here, kv_local, HD)
    offsets = jnp.arange(BLOCK, dtype=jnp.int32)

    def absorb(state, q_four, mask, keys, values):
        top, total, acc = state
        scores = (
            jnp.einsum("qgjd,kgd->qgjk", q_four, keys, preferred_element_type=jnp.float32) * scale
        )
        wide = mask[:, None, None, :]
        fresh_top = jnp.maximum(top, jnp.max(jnp.where(wide, scores, -1e30), -1))
        probs = jnp.where(wide, jnp.exp(scores - fresh_top[..., None]), 0.0)
        factor = jnp.exp(top - fresh_top)
        total = total * factor + jnp.sum(probs, -1)
        acc = acc * factor[..., None] + jnp.einsum(
            "qgjk,kgd->qgjd", probs.astype(jnp.bfloat16), values, preferred_element_type=jnp.float32
        )
        return (fresh_top, total, acc)

    def attend(q_rows, row_ids, state, request):
        count = q_rows.shape[0]
        q_four = q_rows.reshape(count, kv_local, grp, HD)
        q_req = row_ids // tok
        q_index = row_ids % tok
        limit = lax.dynamic_index_in_dim(history_len, request, 0, keepdims=False)
        own_k = lax.dynamic_index_in_dim(grouped_k, request, 0, keepdims=False)
        own_v = lax.dynamic_index_in_dim(grouped_v, request, 0, keepdims=False)
        own_base = lax.dynamic_index_in_dim(grouped_base, request, 0, keepdims=False)

        def visit(carry, item):
            keys, values, base = item
            mask = jnp.broadcast_to((base + offsets < limit)[None, :], (count, BLOCK))
            return (absorb(carry, q_four, mask, keys, values), None)

        state, _ = lax.scan(visit, state, (own_k, own_v, own_base))
        mask = (new_req[None, :] == q_req[:, None]) & (new_index[None, :] <= q_index[:, None])
        return absorb(state, q_four, mask, fresh_k, fresh_v)

    all_queries = lax.all_gather(queries, "ctx", axis=0, tiled=True)
    pieces = []
    for request in range(REQS):
        rows = request * tok + jnp.arange(tok, dtype=jnp.int32)
        pieces.append(
            attend(
                all_queries[request * tok : (request + 1) * tok],
                rows,
                (
                    jnp.full((tok, kv_local, grp), -1e30, jnp.float32),
                    jnp.zeros((tok, kv_local, grp), jnp.float32),
                    jnp.zeros((tok, kv_local, grp, HD), jnp.float32),
                ),
                jnp.int32(request),
            )
        )
    top = jnp.concatenate([p[0] for p in pieces], 0)
    total = jnp.concatenate([p[1] for p in pieces], 0)
    acc = jnp.concatenate([p[2] for p in pieces], 0)
    live = total > 0
    safe = jnp.where(live, total, 1.0)
    part_out = (acc / safe[..., None]).reshape(here * parts, q_local * HD)
    part_lse = jnp.where(live, top + jnp.log(safe), -1e30).reshape(here * parts, q_local)
    got_out, got_lse = (
        lax.all_to_all(part_out, "ctx", split_axis=0, concat_axis=0, tiled=True),
        lax.all_to_all(part_lse, "ctx", split_axis=0, concat_axis=0, tiled=True),
    )
    got_out = got_out.reshape(parts, here, q_local, HD)
    got_lse = got_lse.reshape(parts, here, q_local)
    peak = jnp.max(got_lse, 0)
    weight = jnp.exp(got_lse - peak[None])
    merged = jnp.sum(weight[..., None] * got_out, 0) / jnp.sum(weight, 0)[..., None]
    return merged.reshape(here, q_local * HD)


def solution(mesh):
    placed = (
        P(("rep", "ctx"), "tp"),
        P(("rep", "ctx"), "tp"),
        P(("rep", "ctx"), "tp"),
        P(("rep", "ctx"), "tp"),
        P(("rep", "ctx"), "tp"),
        P(("rep", "ctx")),
        P("rep"),
    )
    return jax.shard_map(
        local, mesh=mesh, in_specs=placed, out_specs=P(("rep", "ctx"), "tp"), check_vma=False
    )
```

profile of v0, /device:TPU:16, one launch (start us, length us, event | category | flops | bytes accessed | tf_op | source)
XLA Modules:
  0.0 413.5 jit_solution(16378168843022642470)
XLA Ops:
  17.9 67.2 %all-gather.2.cloned.1.call-done = bf16[1024,1024]{1,0:T(8,128)(2,1)} async-done(((bf16[64,1024]{1,0:T(8,128)(2,1)}), bf16[1024,1024]{1,0:T(8,128)(2,1)}) %all-gather.2.cloned.1.call-update) | async-done | bytes 2097168 | tf_op jit(solution)/shard_map/all_gather | solution.py:76
  90.9 94.0 %while.30 = (s32[]{:T(128)}, f32[512,1,8]{0,2,1:T(8,128)S(1)}, f32[512,1,8]{0,2,1:T(8,128)S(1)}, f32[512,1,8,128]{0,3,2,1:T(8,128)}, s32[8]{0:T(128)S(1)}, /*ind...) while((s32[]{:T(128)}, f32[512,1,8]{0,2,1:T(8,128)S(1)}, ...), condition=%wide.region_4.5_spmd.clone, body=%wide.region_1.4_spmd.clone.sunk | while | flops 550003200 | bytes 34998440 | solution.py:72
  96.3 4.8 %bitcast_add_fusion.13 = f32[512,1,8,128]{0,3,2,1:T(8,128)} fusion(f32[512,1,8,128]{0,3,2,1:T(8,128)} %get-tuple-element.497, f32[256,512,8]{1,0,2:T(8,128)} %get-tuple-element.435, f32[512,8]{0,1:T(8,128)S(1)} %bitcast.300, pred[256]{0:T(512)(128)(4,1)S(1)} %fusion.111, f32[512,8]{0,1:T(8,128)S(1)} %get-tuple-element.436, pred[]{:T(512)S(6)} %compare.40, ...), kind=kOutput, calls=%fused_computation.14.clone.1 | convolution fusion | flops 274202624 | bytes 8487681 | tf_op jit(solution)/shard_map/while/body/eval_jaxpr/qgjk,kgd->qgjd/dot_general | solution.py:52
  107.5 5.5 %bitcast_add_fusion.13 = f32[512,1,8,128]{0,3,2,1:T(8,128)} fusion(f32[512,1,8,128]{0,3,2,1:T(8,128)} %get-tuple-element.497, f32[256,512,8]{1,0,2:T(8,128)} %get-tuple-element.435, f32[512,8]{0,1:T(8,128)S(1)} %bitcast.300, pred[256]{0:T(512)(128)(4,1)S(1)} %fusion.111, f32[512,8]{0,1:T(8,128)S(1)} %get-tuple-element.436, pred[]{:T(512)S(6)} %compare.40, ...), kind=kOutput, calls=%fused_computation.14.clone.1 | convolution fusion | flops 274202624 | bytes 8487681 | tf_op jit(solution)/shard_map/while/body/eval_jaxpr/qgjk,kgd->qgjd/dot_general | solution.py:52
  115.8 3.5 fusion.112
  119.3 5.5 %bitcast_add_fusion.13 = f32[512,1,8,128]{0,3,2,1:T(8,128)} fusion(f32[512,1,8,128]{0,3,2,1:T(8,128)} %get-tuple-element.497, f32[256,512,8]{1,0,2:T(8,128)} %get-tuple-element.435, f32[512,8]{0,1:T(8,128)S(1)} %bitcast.300, pred[256]{0:T(512)(128)(4,1)S(1)} %fusion.111, f32[512,8]{0,1:T(8,128)S(1)} %get-tuple-element.436, pred[]{:T(512)S(6)} %compare.40, ...), kind=kOutput, calls=%fused_computation.14.clone.1 | convolution fusion | flops 274202624 | bytes 8487681 | tf_op jit(solution)/shard_map/while/body/eval_jaxpr/qgjk,kgd->qgjd/dot_general | solution.py:52
  131.2 5.5 %bitcast_add_fusion.13 = f32[512,1,8,128]{0,3,2,1:T(8,128)} fusion(f32[512,1,8,128]{0,3,2,1:T(8,128)} %get-tuple-element.497, f32[256,512,8]{1,0,2:T(8,128)} %get-tuple-element.435, f32[512,8]{0,1:T(8,128)S(1)} %bitcast.300, pred[256]{0:T(512)(128)(4,1)S(1)} %fusion.111, f32[512,8]{0,1:T(8,128)S(1)} %get-tuple-element.436, pred[]{:T(512)S(6)} %compare.40, ...), kind=kOutput, calls=%fused_computation.14.clone.1 | convolution fusion | flops 274202624 | bytes 8487681 | tf_op jit(solution)/shard_map/while/body/eval_jaxpr/qgjk,kgd->qgjd/dot_general | solution.py:52
  139.5 3.5 fusion.112
  143.0 5.5 %bitcast_add_fusion.13 = f32[512,1,8,128]{0,3,2,1:T(8,128)} fusion(f32[512,1,8,128]{0,3,2,1:T(8,128)} %get-tuple-element.497, f32[256,512,8]{1,0,2:T(8,128)} %get-tuple-element.435, f32[512,8]{0,1:T(8,128)S(1)} %bitcast.300, pred[256]{0:T(512)(128)(4,1)S(1)} %fusion.111, f32[512,8]{0,1:T(8,128)S(1)} %get-tuple-element.436, pred[]{:T(512)S(6)} %compare.40, ...), kind=kOutput, calls=%fused_computation.14.clone.1 | convolution fusion | flops 274202624 | bytes 8487681 | tf_op jit(solution)/shard_map/while/body/eval_jaxpr/qgjk,kgd->qgjd/dot_general | solution.py:52
  154.8 5.5 %bitcast_add_fusion.13 = f32[512,1,8,128]{0,3,2,1:T(8,128)} fusion(f32[512,1,8,128]{0,3,2,1:T(8,128)} %get-tuple-element.497, f32[256,512,8]{1,0,2:T(8,128)} %get-tuple-element.435, f32[512,8]{0,1:T(8,128)S(1)} %bitcast.300, pred[256]{0:T(512)(128)(4,1)S(1)} %fusion.111, f32[512,8]{0,1:T(8,128)S(1)} %get-tuple-element.436, pred[]{:T(512)S(6)} %compare.40, ...), kind=kOutput, calls=%fused_computation.14.clone.1 | convolution fusion | flops 274202624 | bytes 8487681 | tf_op jit(solution)/shard_map/while/body/eval_jaxpr/qgjk,kgd->qgjd/dot_general | solution.py:52
  163.1 3.5 fusion.112
  166.7 5.5 %bitcast_add_fusion.13 = f32[512,1,8,128]{0,3,2,1:T(8,128)} fusion(f32[512,1,8,128]{0,3,2,1:T(8,128)} %get-tuple-element.497, f32[256,512,8]{1,0,2:T(8,128)} %get-tuple-element.435, f32[512,8]{0,1:T(8,128)S(1)} %bitcast.300, pred[256]{0:T(512)(128)(4,1)S(1)} %fusion.111, f32[512,8]{0,1:T(8,128)S(1)} %get-tuple-element.436, pred[]{:T(512)S(6)} %compare.40, ...), kind=kOutput, calls=%fused_computation.14.clone.1 | convolution fusion | flops 274202624 | bytes 8487681 | tf_op jit(solution)/shard_map/while/body/eval_jaxpr/qgjk,kgd->qgjd/dot_general | solution.py:52
  178.5 5.5 %bitcast_add_fusion.13 = f32[512,1,8,128]{0,3,2,1:T(8,128)} fusion(f32[512,1,8,128]{0,3,2,1:T(8,128)} %get-tuple-element.497, f32[256,512,8]{1,0,2:T(8,128)} %get-tuple-element.435, f32[512,8]{0,1:T(8,128)S(1)} %bitcast.300, pred[256]{0:T(512)(128)(4,1)S(1)} %fusion.111, f32[512,8]{0,1:T(8,128)S(1)} %get-tuple-element.436, pred[]{:T(512)S(6)} %compare.40, ...), kind=kOutput, calls=%fused_computation.14.clone.1 | convolution fusion | flops 274202624 | bytes 8487681 | tf_op jit(solution)/shard_map/while/body/eval_jaxpr/qgjk,kgd->qgjd/dot_general | solution.py:52
  194.8 81.7 %while.31 = (s32[]{:T(128)}, f32[512,1,8]{0,2,1:T(8,128)S(1)}, f32[512,1,8]{0,2,1:T(8,128)S(1)}, f32[512,1,8,128]{0,3,2,1:T(8,128)S(1)}, s32[8]{0:T(128)S(1)}, /...) while((s32[]{:T(128)}, f32[512,1,8]{0,2,1:T(8,128)S(1)}, ...), condition=%wide.region_10.11_spmd.clone, body=%wide.region_7.10_spmd.clone.sunk | while | flops 550003200 | bytes 34998440 | solution.py:72
  196.8 3.5 fusion.117
  200.4 3.7 bitcast_add_fusion.15
  207.0 3.5 fusion.117
  210.6 3.7 bitcast_add_fusion.15
  220.8 3.7 bitcast_add_fusion.15
  231.0 3.7 bitcast_add_fusion.15
  241.2 3.7 bitcast_add_fusion.15
  251.4 3.7 bitcast_add_fusion.15
  261.7 3.7 bitcast_add_fusion.15
  271.9 3.7 bitcast_add_fusion.15
  284.3 5.3 %all-to-all-start = ((f32[16,1,512]{2,1,0:T(1,128)}), f32[16,1,512]{2,1,0:T(1,128)S(1)}, u32[]{:S(2)}, u32[]{:S(2)}) async-start(f32[16,1,512]{2,1,0:T(1,128)} %reshape.493), calls=%async_computation | async-start | bytes 65536 | tf_op jit(solution)/shard_map/all_to_all | solution.py:101
  289.7 4.1 pad_maximum_fusion
  296.6 4.9 %div.79 = f32[16,64,1024]{2,1,0:T(8,128)} reshape(f32[1024,8,128]{2,1,0:T(8,128)} %div.78) | data formatting | bytes 8388608 | tf_op jit(solution)/shard_map/div | solution.py:97
  301.5 6.9 %div.80 = f32[16,64,1024]{2,1,0:T(8,128)} divide(f32[16,64,1024]{2,1,0:T(8,128)} %bitcast.299, f32[16,64,1024]{2,1,0:T(8,128)} %div.79) | non-fusion elementwise | flops 1048576 | bytes 12582912 | tf_op jit(solution)/shard_map/div | solution.py:97
  308.3 8.2 %all-to-all-start.1 = ((f32[16,64,1024]{2,1,0:T(8,128)}), f32[16,64,1024]{2,1,0:T(8,128)}, u32[]{:S(2)}, u32[]{:S(2)}) async-start(f32[16,64,1024]{2,1,0:T(8,128)} %div.80), calls=%async_computation.1 | async-start | bytes 8388608 | tf_op jit(solution)/shard_map/all_to_all | solution.py:100
  320.7 4.9 %mul.112 = f32[16,64,1024]{2,1,0:T(8,128)} reshape(f32[16,64,8,128]{3,2,1,0:T(8,128)} %mul.111) | data formatting | bytes 8388608 | tf_op jit(solution)/shard_map/mul | solution.py:107
  325.7 75.8 %all-to-all-done.1 = f32[16,64,1024]{2,1,0:T(8,128)} async-done(((f32[16,64,1024]{2,1,0:T(8,128)}), f32[16,64,1024]{2,1,0:T(8,128)}, u32[]{:S(2)}, u32[]{:S(2)}) %all-to-all-start.1) | async-done | bytes 4194336 | tf_op jit(solution)/shard_map/all_to_all | solution.py:100
  401.5 4.3 %multiply_reduce_fusion = f32[64,1024]{1,0:T(8,128)S(1)} fusion(f32[16,64,1024]{2,1,0:T(8,128)} %mul.112, f32[16,64,1024]{2,1,0:T(8,128)} %all-to-all-done.1), kind=kLoop, calls=%fused_computation.70 | loop fusion | flops 2031616 | bytes 8650752 | tf_op jit(solution)/shard_map/reduce_sum | solution.py:107
  (216 shorter events, 127.1 us)
Async XLA Ops:
  6.5 3.4 copy-start
  6.5 7.1 %copy-start.9 = (s32[2]{0:T(128)S(1)}, s32[2]{0:T(128)}, u32[]{:S(2)}) copy-start(s32[2]{0:T(128)} %param.17) | copy-start | bytes 28
  6.5 78.6 %all-gather.2.cloned.1.call-start = ((), (), s32[]{:S(2)}) async-start(), calls=%async_computation.2 | async-start | bytes 2228224 | tf_op jit(solution)/shard_map/all_gather | solution.py:76
  90.8 94.1 %copy-start.7 = (bf16[64,128]{1,0:T(8,128)(2,1)S(1)}, bf16[64,128]{1,0:T(8,128)(2,1)}, u32[]{:S(2)}) copy-start(bf16[64,128]{1,0:T(8,128)(2,1)} %param.12) | copy-start | bytes 49156
  90.8 96.0 %copy-start.8 = (bf16[64,128]{1,0:T(8,128)(2,1)S(1)}, bf16[64,128]{1,0:T(8,128)(2,1)}, u32[]{:S(2)}) copy-start(bf16[64,128]{1,0:T(8,128)(2,1)} %param.13) | copy-start | bytes 49156
  96.3 4.8 %copy-start.2 = (f32[256,512,8]{1,0,2:T(8,128)S(1)}, f32[256,512,8]{1,0,2:T(8,128)}, u32[]{:S(2)}) copy-start(f32[256,512,8]{1,0,2:T(8,128)} %get-tuple-element.435) | copy-start | bytes 12582916 | tf_op jit(solution)/shard_map/while
  107.5 5.5 %copy-start.2 = (f32[256,512,8]{1,0,2:T(8,128)S(1)}, f32[256,512,8]{1,0,2:T(8,128)}, u32[]{:S(2)}) copy-start(f32[256,512,8]{1,0,2:T(8,128)} %get-tuple-element.435) | copy-start | bytes 12582916 | tf_op jit(solution)/shard_map/while
  119.3 5.5 %copy-start.2 = (f32[256,512,8]{1,0,2:T(8,128)S(1)}, f32[256,512,8]{1,0,2:T(8,128)}, u32[]{:S(2)}) copy-start(f32[256,512,8]{1,0,2:T(8,128)} %get-tuple-element.435) | copy-start | bytes 12582916 | tf_op jit(solution)/shard_map/while
  131.1 5.5 %copy-start.2 = (f32[256,512,8]{1,0,2:T(8,128)S(1)}, f32[256,512,8]{1,0,2:T(8,128)}, u32[]{:S(2)}) copy-start(f32[256,512,8]{1,0,2:T(8,128)} %get-tuple-element.435) | copy-start | bytes 12582916 | tf_op jit(solution)/shard_map/while
  143.0 5.5 %copy-start.2 = (f32[256,512,8]{1,0,2:T(8,128)S(1)}, f32[256,512,8]{1,0,2:T(8,128)}, u32[]{:S(2)}) copy-start(f32[256,512,8]{1,0,2:T(8,128)} %get-tuple-element.435) | copy-start | bytes 12582916 | tf_op jit(solution)/shard_map/while
  154.8 5.5 %copy-start.2 = (f32[256,512,8]{1,0,2:T(8,128)S(1)}, f32[256,512,8]{1,0,2:T(8,128)}, u32[]{:S(2)}) copy-start(f32[256,512,8]{1,0,2:T(8,128)} %get-tuple-element.435) | copy-start | bytes 12582916 | tf_op jit(solution)/shard_map/while
  166.6 5.5 %copy-start.2 = (f32[256,512,8]{1,0,2:T(8,128)S(1)}, f32[256,512,8]{1,0,2:T(8,128)}, u32[]{:S(2)}) copy-start(f32[256,512,8]{1,0,2:T(8,128)} %get-tuple-element.435) | copy-start | bytes 12582916 | tf_op jit(solution)/shard_map/while
  178.5 5.5 %copy-start.2 = (f32[256,512,8]{1,0,2:T(8,128)S(1)}, f32[256,512,8]{1,0,2:T(8,128)}, u32[]{:S(2)}) copy-start(f32[256,512,8]{1,0,2:T(8,128)} %get-tuple-element.435) | copy-start | bytes 12582916 | tf_op jit(solution)/shard_map/while
  184.9 2.0 copy-start.4
  188.8 3.0 copy-start.6
  200.3 3.7 copy-start.3
  210.6 3.7 copy-start.3
  220.8 3.7 copy-start.3
  231.0 3.7 copy-start.3
  241.2 3.7 copy-start.3
  251.4 3.7 copy-start.3
  261.6 3.7 copy-start.3
  271.9 3.7 copy-start.3
  280.3 9.3 %copy-start.5 = (f32[512,1024]{1,0:T(8,128)S(1)}, f32[512,1024]{1,0:T(8,128)}, u32[]{:S(2)}) copy-start(f32[512,1024]{1,0:T(8,128)} %copy.56) | copy-start | bytes 6291460
  284.3 24.0 %all-to-all-start = ((f32[16,1,512]{2,1,0:T(1,128)}), f32[16,1,512]{2,1,0:T(1,128)S(1)}, u32[]{:S(2)}, u32[]{:S(2)}) async-start(f32[16,1,512]{2,1,0:T(1,128)} %reshape.493), calls=%async_computation | async-start | bytes 65536 | tf_op jit(solution)/shard_map/all_to_all | solution.py:101
  308.3 93.1 %all-to-all-start.1 = ((f32[16,64,1024]{2,1,0:T(8,128)}), f32[16,64,1024]{2,1,0:T(8,128)}, u32[]{:S(2)}, u32[]{:S(2)}) async-start(f32[16,64,1024]{2,1,0:T(8,128)} %div.80), calls=%async_computation.1 | async-start | bytes 8388608 | tf_op jit(solution)/shard_map/all_to_all | solution.py:100
  325.6 81.1 %copy-start.1 = (bf16[4096,128]{1,0:T(8,128)(2,1)S(1)}, bf16[4096,128]{1,0:T(8,128)(2,1)}, u32[]{:S(2)}) copy-start(bf16[4096,128]{1,0:T(8,128)(2,1)} %param.14) | copy-start | bytes 3145732
Sparse Core Ops, SparseCore 0:
  9.2 75.9 all-gather.1
where the time goes:
time: 416 us; the launch traced here: 414 us
  waiting for transfers between devices  144 us (35%)
  matrix products  136 us (33%)
  other arithmetic  54.7 us (13%)
  local copies, waits for them, and re-layouts  51.1 us (12%)
  between operations  13.7 us (3%)
  starting transfers between devices  13.5 us (3%)
    dot_general x18, matrix products, absorb(): jnp.einsum('qgjk,kgd->qgjd', probs.astype(jnp.bfloat16), values, preferre...  76.4 us
    all_to_all x1, waiting for transfers between devices, local(): lax.all_to_all(part_out, 'ctx', split_axis=0, concat_axis=0, tiled=True)  75.8 us
    all_gather x1, waiting for transfers between devices, local(): all_queries = lax.all_gather(queries, 'ctx', axis=0, tiled=True)  67.2 us
    dot_general x18, matrix products, absorb(): jnp.einsum('qgjd,kgd->qgjk', q_four, keys, preferred_element_type=jnp.flo...  59.4 us
    lt x16, other arithmetic, visit(): mask = jnp.broadcast_to((base + offsets < limit)[None, :], (count, BLOCK))  20.8 us
    reduce_sum x18, other arithmetic, absorb(): total = total * factor + jnp.sum(probs, -1)  14.5 us
    dynamic_slice x16, local copies, waits for them, and re-layouts, attend(): state, _ = lax.scan(visit, state, (own_k, own_v, own_base))  10.7 us
    unnamed x23, local copies, waits for them, and re-layouts  9.05 us
  transfers between devices with their start and end apart: 3, of which 2 were waited for; matrix products, arithmetic and copies ran while one was open for 9% of the time, Pallas kernels for 0%

commit v1 on v0

v1 whole, which is shorter than its diff:
```python
import functools
import math

import jax
import jax.numpy as jnp
from jax import lax
from jax.experimental import pallas as pl
from jax.experimental.pallas import tpu as pltpu
from jax.sharding import PartitionSpec as P

HD = 128
REQS = 2
BLOCK = 256
LOG2E = math.log2(math.e)
SCALE = LOG2E / math.sqrt(HD)
MESH = pl.DeviceIdType.MESH
RIGHT, LEFT, CROSS = 0, 1, 2
A, B = 0, 1
OWN, OTH = 0, 1
ONES = 16

ORDER = (
    (0, A), (0, B), (7, A), (1, A), (7, B), (1, B), (6, A), (2, A),
    (5, A), (3, A), (4, A), (5, B), (4, B), (3, B), (6, B), (2, B),
)


def dot(a, b, dims):
    return lax.dot_general(a, b, (dims, ((), ())), preferred_element_type=jnp.float32)


def table(values, index):
    out = values[0]
    for k, v in enumerate(values):
        if k:
            out = jnp.where(index == k, v, out)
    return out


def kernel(
    ring, q_in, nk, nv, k_in, v_in, owner, hist, out,
    qbuf, kg, vt, vtn, s0, s1, po, ps, ro, rs, xo, xs,
    q_send, q_recv, p_send, r_recv, x_recv,
):
    here = q_in.shape[0]
    heads = q_in.shape[1] // HD // 2
    rows = here * heads
    hist_rows = kg.shape[1]
    per_req = hist_rows // BLOCK
    blocks = per_req * REQS
    me = lax.axis_index("ctx")
    z, x = lax.div(me, 2), lax.rem(me, 2)
    right = lax.rem(z + 1, ring) * 2 + x
    left = lax.rem(z + ring - 1, ring) * 2 + x
    cross = z * 2 + 1 - x
    target = ({"ctx": right}, {"ctx": left}, {"ctx": cross})

    barrier = pltpu.get_barrier_semaphore()
    for way in (RIGHT, LEFT, CROSS):
        pl.semaphore_signal(barrier, inc=1, device_id=target[way], device_id_type=MESH)

    for g in (A, B):
        for h in range(heads):
            qbuf[0, g, OWN, pl.ds(h * here, here), :] = q_in[:, pl.ds((g * heads + h) * HD, HD)]
    pl.semaphore_wait(barrier, 3)

    def step_to(p, way):
        return (p + (ring - 1, 1, 0)[way]) % ring

    def q_copies(p, g, c, way):
        d = step_to(p, way)
        e = OTH if way == CROSS else c
        return [
            pltpu.make_async_remote_copy(
                src_ref=qbuf.at[p, g, c],
                dst_ref=qbuf.at[d, g, e],
                send_sem=q_send.at[p, g, c, way],
                recv_sem=q_recv.at[d, g, e],
                device_id=target[way],
                device_id_type=MESH,
            )
        ]

    def q_wait(p, g, c):
        pltpu.make_async_remote_copy(
            src_ref=qbuf.at[p, g, c],
            dst_ref=qbuf.at[p, g, c],
            send_sem=q_send.at[p, g, c, RIGHT],
            recv_sem=q_recv.at[p, g, c],
            device_id=target[RIGHT],
            device_id_type=MESH,
        ).wait_recv()

    def slot(p, way):
        return p if way == RIGHT else (p + 3) % ring

    def z_copies(p, g, c, way):
        d = slot(step_to(p, way), way)
        return [
            pltpu.make_async_remote_copy(
                src_ref=src.at[p, g, c],
                dst_ref=dst.at[way, d, g, c],
                send_sem=p_send.at[p, g, c, k],
                recv_sem=r_recv.at[way, d, g, c, k],
                device_id=target[way],
                device_id_type=MESH,
            )
            for k, (src, dst) in enumerate(((po, ro), (ps, rs)))
        ]

    def z_wait(p, g, c, way):
        d = slot(p, way)
        for k, dst in enumerate((ro, rs)):
            pltpu.make_async_remote_copy(
                src_ref=dst.at[way, d, g, c],
                dst_ref=dst.at[way, d, g, c],
                send_sem=p_send.at[p, g, c, k],
                recv_sem=r_recv.at[way, d, g, c, k],
                device_id=target[way],
                device_id_type=MESH,
            ).wait_recv()

    def x_copies(p, g):
        d = p if g == B else ring
        return [
            pltpu.make_async_remote_copy(
                src_ref=src.at[p, g, OTH],
                dst_ref=dst.at[d],
                send_sem=p_send.at[p, g, OTH, k],
                recv_sem=x_recv.at[d, k],
                device_id=target[CROSS],
                device_id_type=MESH,
            )
            for k, (src, dst) in enumerate(((po, xo), (ps, xs)))
        ]

    def x_wait(p, g):
        d = p if g == B else ring
        for k, dst in enumerate((xo, xs)):
            pltpu.make_async_remote_copy(
                src_ref=dst.at[d],
                dst_ref=dst.at[d],
                send_sem=p_send.at[p, g, OTH, k],
                recv_sem=x_recv.at[d, k],
                device_id=target[CROSS],
                device_id_type=MESH,
            ).wait_recv()

    started = []

    def start(make, *args):
        for copy in make(*args):
            copy.start()
        started.append((make, args))

    def merged(parts):
        tops = [s[...] for _, s in parts]
        peak = functools.reduce(jnp.maximum, tops)
        weights = [jnp.exp2(t - peak) for t in tops]
        total = sum(weights[1:], weights[0])
        share = 1.0 / total
        acc = None
        for (o, _), w in zip(parts, weights):
            term = o[...].astype(jnp.float32) * (w * share)
            acc = term if acc is None else acc + term
        return acc, peak + jnp.log(total) * LOG2E

    def fold(p, g, c, others):
        acc, lse = merged([(po.at[p, g, c], ps.at[p, g, c])] + others)
        po[p, g, c] = acc.astype(po.dtype)
        ps[p, g, c] = lse

    def from_z(p, g, c, way):
        d = slot(p, way)
        return (ro.at[way, d, g, c], rs.at[way, d, g, c])

    def need(p, g, c):
        return [(p, g, c)]

    def q_go(p, g, c, *ways):
        return need(p, g, c) + [
            lambda way=way: start(q_copies, p, g, c, way) for way in ways
        ]

    def z_go(p, g, c, way, take=True):
        def run():
            if take:
                z_wait(p, g, c, way)
                fold(p, g, c, [from_z(p, g, c, way)])
            start(z_copies, p, g, c, way)

        return [run]

    def x_go(p):
        return [lambda: start(x_copies, p, B)]

    def x_take(p):
        def run():
            x_wait(p, B)
            fold(p, B, OWN, [(xo.at[p], xs.at[p])])

        return [run]

    def unit_ready(i):
        if i >= len(ORDER):
            return []
        p, g = ORDER[i]
        return need(p, g, OWN) + need(p, g, OTH)

    events = {i: [] for i in range(-1, len(ORDER))}
    events[-1] += q_go(0, A, OWN, RIGHT, LEFT, CROSS) + q_go(0, B, OWN, RIGHT, LEFT, CROSS)
    events[-1] += q_go(0, A, OTH, RIGHT, LEFT)
    events[0] += q_go(7, A, OWN, RIGHT) + q_go(1, A, OWN, LEFT)
    events[0] += q_go(7, B, OWN, RIGHT, CROSS) + q_go(1, B, OWN, LEFT, CROSS)
    events[1] += x_go(0) + q_go(7, A, OTH, RIGHT) + q_go(1, A, OTH, LEFT)
    events[2] += q_go(6, A, OWN, RIGHT) + q_go(2, A, OWN, LEFT)
    events[3] += q_go(6, B, OWN, RIGHT, CROSS) + q_go(2, B, OWN, LEFT, CROSS)
    events[3] += q_go(6, A, OTH, RIGHT) + q_go(2, A, OTH, LEFT)
    events[4] += x_go(7) + q_go(5, A, OWN, RIGHT)
    events[5] += x_go(1) + q_go(5, B, OWN, RIGHT, CROSS) + q_go(3, B, OWN, CROSS)
    events[6] += q_go(3, A, OTH, LEFT)
    events[8] += q_go(4, B, OWN, CROSS) + x_take(7)
    events[9] += x_take(1)
    events[10] += z_go(4, A, OWN, RIGHT, False) + z_go(4, A, OTH, LEFT, False)
    events[10] += z_go(3, A, OTH, RIGHT, False) + z_go(5, A, OWN, LEFT, False)
    events[11] += x_go(5)
    events[12] += x_go(4) + z_go(3, A, OWN, RIGHT) + z_go(5, A, OTH, LEFT)
    events[13] += x_go(3) + x_take(5) + z_go(5, B, OWN, LEFT, False)
    events[13] += z_go(2, A, OTH, RIGHT) + z_go(6, A, OWN, LEFT)
    events[14] += x_go(6) + x_take(4) + z_go(4, B, OWN, RIGHT, False)
    events[14] += z_go(2, A, OWN, RIGHT) + z_go(6, A, OTH, LEFT)
    events[15] += x_go(2) + z_go(1, A, OTH, RIGHT) + z_go(7, A, OWN, LEFT)
    events[15] += x_take(3) + x_take(6) + z_go(6, B, OWN, LEFT)
    events[15] += z_go(1, A, OWN, RIGHT) + z_go(7, A, OTH, LEFT)
    events[15] += z_go(3, B, OWN, RIGHT)

    def last_a():
        z_wait(0, A, OTH, RIGHT)
        z_wait(0, A, OTH, LEFT)
        fold(0, A, OTH, [from_z(0, A, OTH, RIGHT), from_z(0, A, OTH, LEFT)])
        start(x_copies, 0, A)

    def finish(g, cross_slot):
        for way in (RIGHT, LEFT):
            z_wait(0, g, OWN, way)
        x_wait(0, g)
        acc, _ = merged(
            [
                (po.at[0, g, OWN], ps.at[0, g, OWN]),
                from_z(0, g, OWN, RIGHT),
                from_z(0, g, OWN, LEFT),
                (xo.at[cross_slot], xs.at[cross_slot]),
            ]
        )
        for h in range(heads):
            block = acc[:, h * here : (h + 1) * here]
            out[:, pl.ds((g * heads + h) * HD, HD)] = block.T

    events[15] += [last_a] + z_go(7, B, OWN, LEFT) + x_take(2) + z_go(2, B, OWN, RIGHT)
    events[15] += z_go(1, B, OWN, RIGHT)
    events[15] += [lambda: finish(A, ring), lambda: finish(B, 0)]
    events[-1] += unit_ready(0) + unit_ready(1)
    for i in range(len(ORDER)):
        events[i] += unit_ready(i + 2)
    arrived = {(0, A, OWN), (0, B, OWN)}
    for i in sorted(events):
        resolved = []
        for action in events[i]:
            if not isinstance(action, tuple):
                resolved.append(action)
            elif action not in arrived:
                arrived.add(action)
                resolved.append(functools.partial(q_wait, *action))
        events[i] = resolved

    for action in events[-1][:6]:
        action()
    lane = lax.broadcasted_iota(jnp.int32, (ONES, BLOCK), 1)
    sub = lax.broadcasted_iota(jnp.int32, (BLOCK, HD), 0)
    for r in range(REQS):
        first = None
        for b in range(per_req):
            at, base = 0, 0
            for i in range(blocks):
                here_it_is = lax.div(owner[i], 2 * ring) == r * per_req + b
                at = jnp.where(here_it_is, i, at)
                base = jnp.where(here_it_is, owner[i], base)
            base = lax.rem(base, per_req * 2 * ring) * BLOCK
            keys = k_in[at]
            vals = v_in[at]
            if first is None:
                first = keys
            left_over = hist[r] - base
            seen = sub < left_over
            kg[r, pl.ds(b * BLOCK, BLOCK), :] = jnp.where(seen, keys, first)
            vals = jnp.where(seen, vals, jnp.zeros_like(vals))
            vt[r, pl.ds(0, HD), pl.ds(b * BLOCK, BLOCK)] = vals.T
            vt[r, pl.ds(HD, ONES), pl.ds(b * BLOCK, BLOCK)] = jnp.where(
                lane < left_over, 1.0, 0.0
            ).astype(vt.dtype)
        if r == 0:
            for action in events[-1][6:9]:
                action()
    vtn[pl.ds(0, HD), :] = nv[...].T
    vtn[pl.ds(HD, ONES), :] = jnp.ones((ONES, here), vtn.dtype)
    for action in events[-1][9:]:
        action()

    step_p = [p for p, _ in ORDER]
    step_g = [g for _, g in ORDER]
    key_row = lax.broadcasted_iota(jnp.int32, (here, 2 * rows), 0)
    col = lax.broadcasted_iota(jnp.int32, (1, 2 * rows), 1)

    def place(i):
        if isinstance(i, int):
            return step_p[i], step_g[i]
        return table(step_p, i), table(step_g, i)

    def request_of(p):
        return lax.div(lax.rem(z + p, ring) * REQS, ring)

    def score(i, s):
        p, g = place(i)
        home = lax.rem(z + p, ring)
        r = request_of(p)
        q = qbuf[p, g].reshape(2 * rows, HD)
        s[pl.ds(0, hist_rows), :] = dot(kg[r], q, ((1,), (1,)))
        fresh = dot(nk[...], q, ((1,), (1,)))
        same = r == lax.div(z * REQS, ring)
        own_tok = jnp.where(same, (home * 2 + x) * here, -here)
        oth_tok = jnp.where(same, (home * 2 + 1 - x) * here, -here)
        query = jnp.where(col < rows, own_tok, oth_tok) + lax.rem(col, here)
        s[pl.ds(hist_rows, here), :] = jnp.where(me * here + key_row <= query, fresh, -1e30)

    def absorb(i, s):
        p, g = place(i)
        r = request_of(p)
        top = jnp.max(s[...], axis=0, keepdims=True) * SCALE
        probs = jnp.exp2(s[pl.ds(0, hist_rows), :] * SCALE - top).astype(jnp.bfloat16)
        fresh = jnp.exp2(s[pl.ds(hist_rows, here), :] * SCALE - top).astype(jnp.bfloat16)
        acc = dot(vt[r], probs, ((1,), (0,))) + dot(vtn[...], fresh, ((1,), (0,)))
        total = acc[HD : HD + 1]
        part = (acc[:HD] * (1.0 / total)).astype(po.dtype)
        lse = top + jnp.log(total) * LOG2E
        for c in (OWN, OTH):
            po[p, g, c] = part[:, c * rows : (c + 1) * rows]
            ps[p, g, c] = lse[:, c * rows : (c + 1) * rows]

    def after(h, half):
        for k in range(len(ORDER) // 2 - 1):
            if events[2 * k + half]:

                @pl.when(h == k)
                def _():
                    for action in events[2 * k + half]:
                        action()

    score(0, s0)

    @pl.loop(0, len(ORDER) // 2 - 1)
    def _(h):
        score(2 * h + 1, s1)
        absorb(2 * h, s0)
        after(h, 0)
        score(2 * h + 2, s0)
        absorb(2 * h + 1, s1)
        after(h, 1)

    last = len(ORDER) - 1
    score(last, s1)
    absorb(last - 1, s0)
    for action in events[last - 1]:
        action()
    absorb(last, s1)
    for action in events[last]:
        action()
    for make, args in started:
        for copy in make(*args):
            copy.wait_send()


def local(queries, new_keys, new_values, cache_keys, cache_values, block_owner, history_len):
    here, width = queries.shape
    ring = lax.axis_size("ctx") // 2
    rows = here * (width // HD) // 2
    hist_rows = cache_keys.shape[0] // REQS
    bf, f32 = jnp.bfloat16, jnp.float32
    vmem = pl.BlockSpec(memory_space=pltpu.VMEM)
    smem = pl.BlockSpec(memory_space=pltpu.SMEM)
    dma = pltpu.SemaphoreType.DMA
    all_rows = 4 * rows * ring
    keys = hist_rows + here
    return pl.pallas_call(
        functools.partial(kernel, ring),
        out_shape=jax.ShapeDtypeStruct((here, width), f32),
        in_specs=[vmem] * 5 + [smem] * 2,
        out_specs=vmem,
        scratch_shapes=[
            pltpu.VMEM((ring, 2, 2, rows, HD), bf),
            pltpu.VMEM((REQS, hist_rows, HD), bf),
            pltpu.VMEM((REQS, HD + ONES, hist_rows), bf),
            pltpu.VMEM((HD + ONES, here), bf),
            pltpu.VMEM((keys, 2 * rows), f32),
            pltpu.VMEM((keys, 2 * rows), f32),
            pltpu.VMEM((ring, 2, 2, HD, rows), bf),
            pltpu.VMEM((ring, 2, 2, 1, rows), f32),
            pltpu.VMEM((2, 4, 2, 2, HD, rows), bf),
            pltpu.VMEM((2, 4, 2, 2, 1, rows), f32),
            pltpu.VMEM((ring + 1, HD, rows), bf),
            pltpu.VMEM((ring + 1, 1, rows), f32),
            dma((ring, 2, 2, 3)),
            dma((ring, 2, 2)),
            dma((ring, 2, 2, 2)),
            dma((2, 4, 2, 2, 2)),
            dma((ring + 1, 2)),
        ],
        compiler_params=pltpu.CompilerParams(
            collective_id=0, has_side_effects=True, vmem_limit_bytes=48 * 2**20
        ),
        cost_estimate=pl.CostEstimate(
            flops=4 * all_rows * keys * HD,
            bytes_accessed=8 * hist_rows * HD + 6 * here * width,
            transcendentals=all_rows * keys,
        ),
    )(
        queries,
        new_keys,
        new_values,
        cache_keys.reshape(-1, BLOCK, HD),
        cache_values.reshape(-1, BLOCK, HD),
        block_owner,
        history_len,
    )


def solution(mesh):
    rows = P(("rep", "ctx"), "tp")
    return jax.shard_map(
        local,
        mesh=mesh,
        in_specs=(rows,) * 5 + (P(("rep", "ctx")), P("rep")),
        out_specs=rows,
        check_vma=False,
    )
```

time: 416 us -> 66.5 us (0.16)
  waiting for transfers between devices: 144 us -> 0 us
  matrix products: 136 us -> 0 us
  Pallas kernels: 0 us -> 60 us
  other arithmetic: 54.7 us -> 0 us
  local copies, waits for them, and re-layouts: 51.1 us -> 6.16 us
  between operations: 13.7 us -> 0.02 us
  starting transfers between devices: 13.5 us -> 0 us
    dot_general x36 -> x0, matrix products: 136 us -> none  [the longest x18 76.4 us: absorb(): jnp.einsum('qgjk,kgd->qgjd', probs.astype(jnp.bfloat16), values, preferre...]
    all_to_all x2 -> x0, waiting for transfers between devices: 75.8 us -> none  [the longest x1 75.8 us: local(): lax.all_to_all(part_out, 'ctx', split_axis=0, concat_axis=0, tiled=True)]
    all_gather x1 -> x0, waiting for transfers between devices: 67.2 us -> none  [local(): all_queries = lax.all_gather(queries, 'ctx', axis=0, tiled=True)]
    pallas_call x0 -> x1, Pallas kernels: none -> 60 us  [local(): pl.pallas_call(functools.partial(kernel, ring), out_shape=jax.ShapeDtypeS...]
    lt x16 -> x0, other arithmetic: 20.8 us -> none  [visit(): mask = jnp.broadcast_to((base + offsets < limit)[None, :], (count, BLOCK))]
    reduce_sum x20 -> x0, other arithmetic: 18.8 us -> none  [the longest x18 14.5 us: absorb(): total = total * factor + jnp.sum(probs, -1)]
    all_to_all x2 -> x0, starting transfers between devices: 13.5 us -> none  [the longest x1 8.16 us: local(): lax.all_to_all(part_out, 'ctx', split_axis=0, concat_axis=0, tiled=True)]
    dynamic_slice x19 -> x0, local copies, waits for them, and re-layouts: 12.5 us -> none  [the longest x16 10.7 us: attend(): state, _ = lax.scan(visit, state, (own_k, own_v, own_base))]
  transfers between devices with their start and end apart: 3 -> 0, of which waited for: 2 -> 0; matrix products, arithmetic and copies ran while one was open for 9% -> 0% of each run, Pallas kernels for 0% -> 0%
where the time goes in v1:
time: 66.5 us; the launch traced here: 66.2 us
  Pallas kernels  60 us (90%)
  local copies, waits for them, and re-layouts  6.16 us (9%)
    pallas_call x1, Pallas kernels, local(): pl.pallas_call(functools.partial(kernel, ring), out_shape=jax.ShapeDtypeS...  60 us
    unnamed x15, local copies, waits for them, and re-layouts  6.16 us

profile of v1, /device:TPU:16, one launch (start us, length us, event | category | flops | bytes accessed | tf_op | source)
XLA Modules:
  0.0 66.2 jit_solution(14831183003985225749)
XLA Ops:
  0.0 0.0 copy-start.5
  0.0 0.0 copy-start.6
  0.0 0.7 copy-done.5
  0.7 0.0 copy-done.6
  0.7 0.0 copy-start
  0.7 1.2 %copy-done = bf16[4096,128]{1,0:T(8,128)(2,1)S(1)} copy-done((bf16[4096,128]{1,0:T(8,128)(2,1)S(1)}, bf16[4096,128]{1,0:T(8,128)(2,1)}, u32[]{:S(2)}) %copy-start) | copy-done | bytes 1048600
  1.9 0.0 copy-start.1
  1.9 1.2 %copy-done.1 = bf16[4096,128]{1,0:T(8,128)(2,1)S(1)} copy-done((bf16[4096,128]{1,0:T(8,128)(2,1)S(1)}, bf16[4096,128]{1,0:T(8,128)(2,1)}, u32[]{:S(2)}) %copy-start.1) | copy-done | bytes 1048600
  3.1 0.0 copy-start.2
  3.1 0.9 %copy-done.2 = bf16[64,1024]{1,0:T(8,128)(2,1)S(1)} copy-done((bf16[64,1024]{1,0:T(8,128)(2,1)S(1)}, bf16[64,1024]{1,0:T(8,128)(2,1)}, u32[]{:S(2)}) %copy-start.2) | copy-done | bytes 131096
  4.0 0.0 copy-start.3
  4.0 0.7 %copy-done.3 = bf16[64,128]{1,0:T(8,128)(2,1)S(1)} copy-done((bf16[64,128]{1,0:T(8,128)(2,1)S(1)}, bf16[64,128]{1,0:T(8,128)(2,1)}, u32[]{:S(2)}) %copy-start.3) | copy-done | bytes 16408
  4.7 0.0 copy-start.4
  4.7 0.7 %copy-done.4 = bf16[64,128]{1,0:T(8,128)(2,1)S(1)} copy-done((bf16[64,128]{1,0:T(8,128)(2,1)S(1)}, bf16[64,128]{1,0:T(8,128)(2,1)}, u32[]{:S(2)}) %copy-start.4) | copy-done | bytes 16408
  5.5 60.0 %shard_map.73 = f32[64,1024]{1,0:T(8,128)S(1)} custom-call(bf16[64,1024]{1,0:T(8,128)(2,1)S(1)} %copy-done.2, bf16[64,128]{1,0:T(8,128)(2,1)S(1)} %copy-done.3, bf16[64,128]{1,0:T(8,128)(2,1)S(1)} %copy-done.4, bf16[16,256,128]{2,1,0:T(8,128)(2,1)S(1)} %bitcast.2, bf16[16,256,128]{2,1,0:T(8,128)(2,1)S(1)} %bitcast.3, s32[16]{0:T(128)S(1)} %copy-done.5, ...), custom_call_target="tpu_custom_call" | custom-call | flops 8858370048 | bytes 2490368 | tf_op jit(solution)/shard_map/pallas_call | solution.py:393
  65.5 0.7 %copy.9 = f32[64,1024]{1,0:T(8,128)} copy(f32[64,1024]{1,0:T(8,128)S(1)} %shard_map.73) | data formatting | bytes 524288
Async XLA Ops:
  0.0 0.7 copy-start.5
  0.0 0.7 %copy-start.6 = (s32[2]{0:T(128)S(1)}, s32[2]{0:T(128)}, u32[]{:S(2)}) copy-start(s32[2]{0:T(128)} %hist.1) | copy-start | bytes 28
  0.7 1.2 %copy-start = (bf16[4096,128]{1,0:T(8,128)(2,1)S(1)}, bf16[4096,128]{1,0:T(8,128)(2,1)}, u32[]{:S(2)}) copy-start(bf16[4096,128]{1,0:T(8,128)(2,1)} %param.10) | copy-start | bytes 3145732
  1.9 1.2 %copy-start.1 = (bf16[4096,128]{1,0:T(8,128)(2,1)S(1)}, bf16[4096,128]{1,0:T(8,128)(2,1)}, u32[]{:S(2)}) copy-start(bf16[4096,128]{1,0:T(8,128)(2,1)} %param.11) | copy-start | bytes 3145732
  3.1 0.9 %copy-start.2 = (bf16[64,1024]{1,0:T(8,128)(2,1)S(1)}, bf16[64,1024]{1,0:T(8,128)(2,1)}, u32[]{:S(2)}) copy-start(bf16[64,1024]{1,0:T(8,128)(2,1)} %q_in.1) | copy-start | bytes 393220
  4.0 0.7 %copy-start.3 = (bf16[64,128]{1,0:T(8,128)(2,1)S(1)}, bf16[64,128]{1,0:T(8,128)(2,1)}, u32[]{:S(2)}) copy-start(bf16[64,128]{1,0:T(8,128)(2,1)} %nk.1) | copy-start | bytes 49156
  4.7 0.7 %copy-start.4 = (bf16[64,128]{1,0:T(8,128)(2,1)S(1)}, bf16[64,128]{1,0:T(8,128)(2,1)}, u32[]{:S(2)}) copy-start(bf16[64,128]{1,0:T(8,128)(2,1)} %nv.1) | copy-start | bytes 49156

commit v2 on v1

v2 whole, which is shorter than its diff:
```python
import functools
import math

import jax
import jax.numpy as jnp
from jax import lax
from jax.experimental import pallas as pl
from jax.experimental.pallas import tpu as pltpu
from jax.sharding import PartitionSpec as P

HD = 128
REQS = 2
BLOCK = 256
LOG2E = math.log2(math.e)
SCALE = LOG2E / math.sqrt(HD)
MESH = pl.DeviceIdType.MESH
A, B = 0, 1
OWN, OTH = 0, 1
ONES = 16
Q, S, F = 0, 1, 2

ORDER = (
    (1, 0),
    (7, 0),
    (0, 1),
    (2, 0),
    (7, 1),
    (6, 0),
    (3, 0),
    (5, 0),
    (1, 1),
    (5, 1),
    (4, 0),
    (4, 1),
    (3, 1),
    (6, 1),
    (2, 1),
    (0, 0),
)
BEFORE = (
    ((Q, 0, 0, 0, 1, 1), (Q, 0, 1, 0, 1, 0), (Q, 0, 0, 0, -1, 0), (Q, 0, 0, 0, 1, 0), (Q, 0, 0, 0, -1, 1), (Q, 0, 0, 0, 0, 1), (Q, 0, 1, 0, -1, 0), (Q, 0, 1, 0, 0, 1),),
    (),
    (),
    (),
    (),
    (),
    (),
    (),
    (),
    ((Q, 1, 0, 0, -1, 0), (Q, 7, 0, 1, 1, 0), (Q, 7, 1, 0, 0, 1), (Q, 7, 1, 0, 1, 0), (Q, 1, 0, 1, -1, 0),),
    ((Q, 7, 0, 0, 1, 0),),
)
AFTER = (
    ((Q, 1, 1, 0, -1, 0), (Q, 2, 0, 0, -1, 0), (Q, 1, 1, 0, 0, 1),),
    ((Q, 6, 1, 0, 1, 0), (Q, 6, 0, 1, 1, 0), (Q, 6, 1, 0, 0, 1), (Q, 2, 0, 1, -1, 0),),
    ((Q, 6, 0, 0, 1, 0), (S, 0, 1, 1, 0, 1),),
    ((Q, 2, 1, 0, -2, 0), (Q, 2, 1, 0, 0, 1), (Q, 2, 1, 0, -1, 0),),
    ((Q, 5, 1, 0, 0, 1), (S, 7, 1, 1, 0, 1),),
    ((Q, 5, 0, 1, 1, 0), (Q, 5, 0, 0, 1, 0),),
    ((S, 3, 0, 1, 1, 0), (S, 3, 0, 0, 1, 0), (Q, 4, 1, 0, 0, 1),),
    ((Q, 3, 1, 0, 0, 1), (S, 5, 0, 1, -1, 0), (S, 5, 0, 0, -1, 0),),
    ((S, 1, 1, 1, 0, 1), (F, 7, 1, 0, ((7, 1, 1, 0, 1),)), (S, 7, 1, 0, -1, 0),),
    ((F, 2, 0, 1, ((3, 0, 1, 1, 0),)), (S, 2, 0, 1, 1, 0), (S, 5, 1, 1, 0, 1),),
    ((S, 4, 0, 1, -2, 0), (S, 4, 0, 0, 2, 0),),
    ((S, 4, 1, 1, 0, 1), (F, 1, 1, 0, ((1, 1, 1, 0, 1),)), (S, 1, 1, 0, 1, 0), (F, 6, 0, 0, ((5, 0, 0, -1, 0),)), (S, 6, 0, 0, -1, 0),),
    ((S, 3, 1, 1, 0, 1), (F, 5, 1, 0, ((5, 1, 1, 0, 1),)), (S, 5, 1, 0, -1, 0), (F, 1, 0, 1, ((2, 0, 1, 1, 0),)), (S, 1, 0, 1, 1, 1),),
    ((F, 6, 0, 1, ((4, 0, 1, -2, 0), (5, 0, 1, -1, 0))), (S, 6, 0, 1, -1, 0), (F, 2, 0, 0, ((4, 0, 0, 2, 0), (3, 0, 0, 1, 0))), (S, 2, 0, 0, 1, 0), (S, 6, 1, 1, 0, 1), (F, 4, 1, 0, ((4, 1, 1, 0, 1),)), (S, 4, 1, 0, -2, 0),),
    ((S, 2, 1, 1, 0, 1), (F, 7, 0, 0, ((6, 0, 0, -1, 0),)), (S, 7, 0, 0, -1, 0), (F, 3, 1, 0, ((3, 1, 1, 0, 1),)), (S, 3, 1, 0, 1, 0),),
    ((S, 0, 0, 1, 0, 1),),
    ((F, 7, 0, 1, ((6, 0, 1, -1, 0),)), (S, 7, 0, 1, -1, 1), (F, 6, 1, 0, ((6, 1, 1, 0, 1),)), (F, 1, 0, 0, ((2, 0, 0, 1, 0),)), (S, 1, 0, 0, 1, 0), (F, 6, 1, 0, ((4, 1, 0, -2, 0), (5, 1, 0, -1, 0))), (S, 6, 1, 0, -2, 0), (F, 2, 1, 0, ((2, 1, 1, 0, 1),)), (F, 2, 1, 0, ((3, 1, 0, 1, 0),)), (S, 2, 1, 0, 2, 0),),
)
LAST = (
    ((1, 0, 0, 1, 0), (7, 0, 0, -1, 0), (1, 0, 1, 1, 1), (7, 0, 1, -1, 1), (0, 0, 1, 0, 1),),
    ((2, 1, 0, 2, 0), (1, 1, 0, 1, 0), (6, 1, 0, -2, 0), (7, 1, 0, -1, 0), (0, 1, 1, 0, 1),),
)

MESSAGES = tuple(e[1:] for es in BEFORE + AFTER for e in es if e[0] == S)
QUERIES = tuple(e[1:] for es in BEFORE + AFTER for e in es if e[0] == Q)
PARTNERS = tuple(sorted({m[3:] for m in MESSAGES + QUERIES}))


def dot(a, b, dims):
    return lax.dot_general(a, b, (dims, ((), ())), preferred_element_type=jnp.float32)


def table(values, index):
    out = values[0]
    for k, v in enumerate(values):
        if k:
            out = jnp.where(index == k, v, out)
    return out


def kernel(
    ring, q_in, nk_in, nv_in, k_hbm, v_hbm, owner, hist, out,
    qbuf, nk, nv, k_in, v_in, kg, vt, vtn, s0, s1, po, ps, ro, rs,
    l_sem, q_send, q_recv, p_send, p_recv,
):
    here, width = q_in.shape
    heads = width // HD // 2
    rows = here * heads
    hist_rows = kg.shape[1]
    per_req = hist_rows // BLOCK
    blocks = per_req * REQS
    me = lax.axis_index("ctx")
    z, x = lax.div(me, 2), lax.rem(me, 2)

    def device(steps, cross):
        column = 1 - x if cross else x
        return {"ctx": lax.rem(z + (ring + steps) % ring, ring) * 2 + column}

    loads = [
        (q_in.at[:, pl.ds((g * heads + h) * HD, HD)], qbuf.at[0, g, OWN, pl.ds(h * here, here)])
        for g in (A, B)
        for h in range(heads)
    ]
    own_queries = len(loads)
    loads += [(k_hbm, k_in), (v_hbm, v_in), (nk_in, nk), (nv_in, nv)]
    loads = [pltpu.make_async_copy(a, b, l_sem.at[i]) for i, (a, b) in enumerate(loads)]
    for load in loads:
        load.start()
    barrier = pltpu.get_barrier_semaphore()
    for partner in PARTNERS:
        pl.semaphore_signal(barrier, inc=1, device_id=device(*partner), device_id_type=MESH)
    for load in loads[:own_queries]:
        load.wait()
    pl.semaphore_wait(barrier, len(PARTNERS))

    def q_copy(n):
        p, g, c, steps, cross = QUERIES[n]
        d = (p - steps) % ring
        e = OTH if cross else c
        return pltpu.make_async_remote_copy(
            src_ref=qbuf.at[p, g, c],
            dst_ref=qbuf.at[d, g, e],
            send_sem=q_send.at[n],
            recv_sem=q_recv.at[d, g, e],
            device_id=device(steps, cross),
            device_id_type=MESH,
        )

    def q_wait(p, g, c):
        pltpu.make_async_remote_copy(
            src_ref=qbuf.at[p, g, c],
            dst_ref=qbuf.at[p, g, c],
            send_sem=q_send.at[0],
            recv_sem=q_recv.at[p, g, c],
            device_id=device(*PARTNERS[0]),
            device_id_type=MESH,
        ).wait_recv()

    def p_copies(n):
        p, g, c, steps, cross = MESSAGES[n]
        return [
            pltpu.make_async_remote_copy(
                src_ref=src.at[p, g, c],
                dst_ref=dst.at[n],
                send_sem=p_send.at[n, k],
                recv_sem=p_recv.at[n, k],
                device_id=device(steps, cross),
                device_id_type=MESH,
            )
            for k, (src, dst) in enumerate(((po, ro), (ps, rs)))
        ]

    def merged(parts):
        tops = [s[...] for _, s in parts]
        peak = functools.reduce(jnp.maximum, tops)
        weights = [jnp.exp2(t - peak) for t in tops]
        total = sum(weights[1:], weights[0])
        share = 1.0 / total
        acc = None
        for (o, _), w in zip(parts, weights):
            term = o[...].astype(jnp.float32) * (w * share)
            acc = term if acc is None else acc + term
        return acc, peak + jnp.log(total) * LOG2E

    def take(p, g, c, messages):
        parts = [(po.at[p, g, c], ps.at[p, g, c])]
        for message in messages:
            n = MESSAGES.index(message)
            for copy in p_copies(n):
                copy.wait_recv()
            parts.append((ro.at[n], rs.at[n]))
        return merged(parts)

    def finish(g):
        acc, _ = take(0, g, OWN, LAST[g])
        for h in range(heads):
            out[:, pl.ds((g * heads + h) * HD, HD)] = acc[:, h * here : (h + 1) * here].T

    def act(event):
        kind, *rest = event
        if kind == Q:
            q_copy(QUERIES.index(tuple(rest))).start()
        elif kind == S:
            for copy in p_copies(MESSAGES.index(tuple(rest))):
                copy.start()
        elif kind == F:
            p, g, c, messages = rest
            acc, lse = take(p, g, c, messages)
            po[p, g, c] = acc.astype(po.dtype)
            ps[p, g, c] = lse
        else:
            q_wait(*rest)

    arrived = {(0, A, OWN), (0, B, OWN)}

    def with_waits(events, unit):
        result = []
        needs = [(e, [e[1:4]] if e[0] == Q else []) for e in events]
        if unit < len(ORDER):
            needs.append((None, [ORDER[unit] + (c,) for c in (OWN, OTH)]))
        for event, blocks_of in needs:
            for block in blocks_of:
                if block not in arrived:
                    arrived.add(block)
                    result.append((None,) + block)
            if event is not None:
                result.append(event)
        return result

    none = len(ORDER)
    before = [with_waits(es, none) for es in BEFORE[:-2]]
    before += [with_waits(BEFORE[-2], 0), with_waits(BEFORE[-1], 1)]
    after = [with_waits(es, i + 2) for i, es in enumerate(AFTER)]

    for event in before[0]:
        act(event)
    for load in loads[own_queries:]:
        load.wait()

    lane = lax.broadcasted_iota(jnp.int32, (ONES, BLOCK), 1)
    sub = lax.broadcasted_iota(jnp.int32, (BLOCK, HD), 0)
    parts = len(before) - 3
    for i in range(blocks):
        r, b = i // per_req, i % per_req
        at, base = 0, 0
        for j in range(blocks):
            found = lax.div(owner[j], 2 * ring) == i
            at = jnp.where(found, j, at)
            base = jnp.where(found, owner[j], base)
        base = lax.rem(base, per_req * 2 * ring) * BLOCK
        keys = k_in[at]
        vals = v_in[at]
        if b == 0:
            first = keys
        left_over = hist[r] - base
        seen = sub < left_over
        kg[r, pl.ds(b * BLOCK, BLOCK), :] = jnp.where(seen, keys, first)
        vals = jnp.where(seen, vals, jnp.zeros_like(vals))
        vt[r, pl.ds(0, HD), pl.ds(b * BLOCK, BLOCK)] = vals.T
        vt[r, pl.ds(HD, ONES), pl.ds(b * BLOCK, BLOCK)] = jnp.where(
            lane < left_over, 1.0, 0.0
        ).astype(vt.dtype)
        if (i + 1) * parts % blocks == 0:
            for event in before[(i + 1) * parts // blocks]:
                act(event)
    vtn[pl.ds(0, HD), :] = nv[...].T
    vtn[pl.ds(HD, ONES), :] = jnp.ones((ONES, here), vtn.dtype)
    for event in before[-2]:
        act(event)

    step_p = [p for p, _ in ORDER]
    step_g = [g for _, g in ORDER]
    key_row = lax.broadcasted_iota(jnp.int32, (here, 2 * rows), 0)
    col = lax.broadcasted_iota(jnp.int32, (1, 2 * rows), 1)

    def place(i):
        if isinstance(i, int):
            return step_p[i], step_g[i]
        return table(step_p, i), table(step_g, i)

    def request_of(p):
        return lax.div(lax.rem(z + p, ring) * REQS, ring)

    def score(i, s):
        p, g = place(i)
        home = lax.rem(z + p, ring)
        r = request_of(p)
        q = qbuf[p, g].reshape(2 * rows, HD)
        s[pl.ds(0, hist_rows), :] = dot(kg[r], q, ((1,), (1,)))
        fresh = dot(nk[...], q, ((1,), (1,)))
        same = r == lax.div(z * REQS, ring)
        own_tok = jnp.where(same, (home * 2 + x) * here, -here)
        oth_tok = jnp.where(same, (home * 2 + 1 - x) * here, -here)
        query = jnp.where(col < rows, own_tok, oth_tok) + lax.rem(col, here)
        s[pl.ds(hist_rows, here), :] = jnp.where(me * here + key_row <= query, fresh, -1e30)

    def absorb(i, s):
        p, g = place(i)
        r = request_of(p)
        top = jnp.max(s[...], axis=0, keepdims=True) * SCALE
        probs = jnp.exp2(s[pl.ds(0, hist_rows), :] * SCALE - top).astype(jnp.bfloat16)
        fresh = jnp.exp2(s[pl.ds(hist_rows, here), :] * SCALE - top).astype(jnp.bfloat16)
        acc = dot(vt[r], probs, ((1,), (0,))) + dot(vtn[...], fresh, ((1,), (0,)))
        total = acc[HD : HD + 1]
        part = (acc[:HD] * (1.0 / total)).astype(po.dtype)
        lse = top + jnp.log(total) * LOG2E
        for c in (OWN, OTH):
            po[p, g, c] = part[:, c * rows : (c + 1) * rows]
            ps[p, g, c] = lse[:, c * rows : (c + 1) * rows]

    def react(h, half):
        for k in range(len(ORDER) // 2 - 1):
            if after[2 * k + half]:

                @pl.when(h == k)
                def _():
                    for event in after[2 * k + half]:
                        act(event)

    score(0, s0)
    for event in before[-1]:
        act(event)

    @pl.loop(0, len(ORDER) // 2 - 1)
    def _(h):
        score(2 * h + 1, s1)
        absorb(2 * h, s0)
        react(h, 0)
        score(2 * h + 2, s0)
        absorb(2 * h + 1, s1)
        react(h, 1)

    last = len(ORDER) - 1
    score(last, s1)
    absorb(last - 1, s0)
    for event in after[last - 1]:
        act(event)
    absorb(last, s1)
    for event in after[last] + after[last + 1]:
        act(event)
    finish(A)
    finish(B)
    for n in range(len(QUERIES)):
        q_copy(n).wait_send()
    for n in range(len(MESSAGES)):
        for copy in p_copies(n):
            copy.wait_send()


def local(queries, new_keys, new_values, cache_keys, cache_values, block_owner, history_len):
    here, width = queries.shape
    ring = lax.axis_size("ctx") // 2
    heads = width // HD
    rows = here * heads // 2
    slots = cache_keys.shape[0]
    hist_rows = slots // REQS
    bf, f32 = jnp.bfloat16, jnp.float32
    hbm = pl.BlockSpec(memory_space=pl.ANY)
    smem = pl.BlockSpec(memory_space=pltpu.SMEM)
    dma = pltpu.SemaphoreType.DMA
    all_rows = 4 * rows * ring
    keys = hist_rows + here
    return pl.pallas_call(
        functools.partial(kernel, ring),
        out_shape=jax.ShapeDtypeStruct((here, width), f32),
        in_specs=[hbm] * 5 + [smem] * 2,
        out_specs=pl.BlockSpec(memory_space=pltpu.VMEM),
        scratch_shapes=[
            pltpu.VMEM((ring, 2, 2, rows, HD), bf),
            pltpu.VMEM((here, HD), bf),
            pltpu.VMEM((here, HD), bf),
            pltpu.VMEM((slots // BLOCK, BLOCK, HD), bf),
            pltpu.VMEM((slots // BLOCK, BLOCK, HD), bf),
            pltpu.VMEM((REQS, hist_rows, HD), bf),
            pltpu.VMEM((REQS, HD + ONES, hist_rows), bf),
            pltpu.VMEM((HD + ONES, here), bf),
            pltpu.VMEM((keys, 2 * rows), f32),
            pltpu.VMEM((keys, 2 * rows), f32),
            pltpu.VMEM((ring, 2, 2, HD, rows), bf),
            pltpu.VMEM((ring, 2, 2, 1, rows), f32),
            pltpu.VMEM((len(MESSAGES), HD, rows), bf),
            pltpu.VMEM((len(MESSAGES), 1, rows), f32),
            dma((heads + 4,)),
            dma((len(QUERIES),)),
            dma((ring, 2, 2)),
            dma((len(MESSAGES), 2)),
            dma((len(MESSAGES), 2)),
        ],
        compiler_params=pltpu.CompilerParams(
            collective_id=0, has_side_effects=True, vmem_limit_bytes=52 * 2**20
        ),
        cost_estimate=pl.CostEstimate(
            flops=4 * all_rows * keys * HD,
            bytes_accessed=4 * slots * HD + 6 * here * width,
            transcendentals=all_rows * keys,
        ),
    )(
        queries,
        new_keys,
        new_values,
        cache_keys.reshape(-1, BLOCK, HD),
        cache_values.reshape(-1, BLOCK, HD),
        block_owner,
        history_len,
    )


def solution(mesh):
    rows = P(("rep", "ctx"), "tp")
    return jax.shard_map(
        local,
        mesh=mesh,
        in_specs=(rows,) * 5 + (P(("rep", "ctx")), P("rep")),
        out_specs=rows,
        check_vma=False,
    )
```

time: 66.5 us -> 57.8 us (0.87)
  Pallas kernels: 60 us -> 52.6 us
  local copies, waits for them, and re-layouts: 6.16 us -> 4.94 us
    pallas_call x1, Pallas kernels: 60 us -> 52.6 us  [local(): pl.pallas_call(functools.partial(kernel, ring), out_shape=jax.ShapeDtypeS...]
    unnamed x15 -> x13, local copies, waits for them, and re-layouts: 6.16 us -> 4.94 us
where the time goes in v2:
time: 57.8 us; the launch traced here: 57.5 us
  Pallas kernels  52.6 us (91%)
  local copies, waits for them, and re-layouts  4.94 us (9%)
    pallas_call x1, Pallas kernels, local(): pl.pallas_call(functools.partial(kernel, ring), out_shape=jax.ShapeDtypeS...  52.6 us
    unnamed x13, local copies, waits for them, and re-layouts  4.94 us

profile of v2, /device:TPU:16, one launch (start us, length us, event | category | flops | bytes accessed | tf_op | source)
XLA Modules:
  0.0 57.5 jit_solution(9773369033173554624)
XLA Ops:
  0.0 0.0 copy-start.4
  0.0 0.0 copy-start.5
  0.0 0.7 %copy-done.4 = s32[16]{0:T(128)S(1)} copy-done((s32[16]{0:T(128)S(1)}, s32[16]{0:T(128)}, u32[]{:S(2)}) %copy-start.4) | copy-done | bytes 88
  0.7 0.0 copy-done.5
  0.7 0.0 copy-start
  0.7 1.2 %copy-done = bf16[4096,128]{1,0:T(8,128)(2,1)S(1)} copy-done((bf16[4096,128]{1,0:T(8,128)(2,1)S(1)}, bf16[4096,128]{1,0:T(8,128)(2,1)}, u32[]{:S(2)}) %copy-start) | copy-done | bytes 1048600
  1.9 0.0 copy-start.1
  1.9 0.9 %copy-done.1 = bf16[64,1024]{1,0:T(8,128)(2,1)S(1)} copy-done((bf16[64,1024]{1,0:T(8,128)(2,1)S(1)}, bf16[64,1024]{1,0:T(8,128)(2,1)}, u32[]{:S(2)}) %copy-start.1) | copy-done | bytes 131096
  2.8 0.0 copy-start.2
  2.8 0.7 %copy-done.2 = bf16[64,128]{1,0:T(8,128)(2,1)S(1)} copy-done((bf16[64,128]{1,0:T(8,128)(2,1)S(1)}, bf16[64,128]{1,0:T(8,128)(2,1)}, u32[]{:S(2)}) %copy-start.2) | copy-done | bytes 16408
  3.5 0.0 copy-start.3
  3.5 0.7 %copy-done.3 = bf16[64,128]{1,0:T(8,128)(2,1)S(1)} copy-done((bf16[64,128]{1,0:T(8,128)(2,1)S(1)}, bf16[64,128]{1,0:T(8,128)(2,1)}, u32[]{:S(2)}) %copy-start.3) | copy-done | bytes 16408
  4.2 52.6 %shard_map.73 = f32[64,1024]{1,0:T(8,128)S(1)} custom-call(bf16[64,1024]{1,0:T(8,128)(2,1)S(1)} %copy-done.1, bf16[64,128]{1,0:T(8,128)(2,1)S(1)} %copy-done.2, bf16[64,128]{1,0:T(8,128)(2,1)S(1)} %copy-done.3, bf16[16,256,128]{2,1,0:T(8,128)(2,1)S(1)} %bitcast.2, bf16[16,256,128]{2,1,0:T(8,128)(2,1)} %bitcast.3, s32[16]{0:T(128)S(1)} %copy-done.4, ...), custom_call_target="tpu_custom_call" | custom-call | flops 8858370048 | bytes 2490368 | tf_op jit(solution)/shard_map/pallas_call | solution.py:356
  56.8 0.7 %copy.9 = f32[64,1024]{1,0:T(8,128)} copy(f32[64,1024]{1,0:T(8,128)S(1)} %shard_map.73) | data formatting | bytes 524288
Async XLA Ops:
  0.0 0.7 %copy-start.4 = (s32[16]{0:T(128)S(1)}, s32[16]{0:T(128)}, u32[]{:S(2)}) copy-start(s32[16]{0:T(128)} %owner.1) | copy-start | bytes 196
  0.0 0.7 %copy-start.5 = (s32[2]{0:T(128)S(1)}, s32[2]{0:T(128)}, u32[]{:S(2)}) copy-start(s32[2]{0:T(128)} %hist.1) | copy-start | bytes 28
  0.7 1.2 %copy-start = (bf16[4096,128]{1,0:T(8,128)(2,1)S(1)}, bf16[4096,128]{1,0:T(8,128)(2,1)}, u32[]{:S(2)}) copy-start(bf16[4096,128]{1,0:T(8,128)(2,1)} %param.10) | copy-start | bytes 3145732
  1.9 0.9 %copy-start.1 = (bf16[64,1024]{1,0:T(8,128)(2,1)S(1)}, bf16[64,1024]{1,0:T(8,128)(2,1)}, u32[]{:S(2)}) copy-start(bf16[64,1024]{1,0:T(8,128)(2,1)} %q_in.1) | copy-start | bytes 393220
  2.8 0.7 %copy-start.2 = (bf16[64,128]{1,0:T(8,128)(2,1)S(1)}, bf16[64,128]{1,0:T(8,128)(2,1)}, u32[]{:S(2)}) copy-start(bf16[64,128]{1,0:T(8,128)(2,1)} %nk_in.1) | copy-start | bytes 49156
  3.5 0.7 %copy-start.3 = (bf16[64,128]{1,0:T(8,128)(2,1)S(1)}, bf16[64,128]{1,0:T(8,128)(2,1)}, u32[]{:S(2)}) copy-start(bf16[64,128]{1,0:T(8,128)(2,1)} %nv_in.1) | copy-start | bytes 49156

commit v3 on v2

--- a/solution.py
+++ b/solution.py
@@ -92,8 +92,8 @@
 
 
 def kernel(
-    ring, q_in, nk_in, nv_in, k_hbm, v_hbm, owner, hist, out,
-    qbuf, nk, nv, k_in, v_in, kg, vt, vtn, s0, s1, po, ps, ro, rs,
+    ring, q_in, nk_in, nv_in, k_hbm, v_hbm, owner_in, hist_in, out,
+    qbuf, owner, hist, nk, nv, k_in, v_in, kg, vt, vtn, s0, s1, po, ps, ro, rs,
     l_sem, q_send, q_recv, p_send, p_recv,
 ):
     here, width = q_in.shape
@@ -115,6 +115,7 @@
         for h in range(heads)
     ]
     own_queries = len(loads)
+    loads += [(owner_in, owner), (hist_in, hist)]
     loads += [(k_hbm, k_in), (v_hbm, v_in), (nk_in, nk), (nv_in, nv)]
     loads = [pltpu.make_async_copy(a, b, l_sem.at[i]) for i, (a, b) in enumerate(loads)]
     for load in loads:
@@ -348,18 +349,19 @@
     slots = cache_keys.shape[0]
     hist_rows = slots // REQS
     bf, f32 = jnp.bfloat16, jnp.float32
-    hbm = pl.BlockSpec(memory_space=pl.ANY)
-    smem = pl.BlockSpec(memory_space=pltpu.SMEM)
+    hbm = pl.BlockSpec(memory_space=pltpu.HBM)
     dma = pltpu.SemaphoreType.DMA
     all_rows = 4 * rows * ring
     keys = hist_rows + here
     return pl.pallas_call(
         functools.partial(kernel, ring),
         out_shape=jax.ShapeDtypeStruct((here, width), f32),
-        in_specs=[hbm] * 5 + [smem] * 2,
+        in_specs=[hbm] * 7,
         out_specs=pl.BlockSpec(memory_space=pltpu.VMEM),
         scratch_shapes=[
             pltpu.VMEM((ring, 2, 2, rows, HD), bf),
+            pltpu.SMEM(block_owner.shape, jnp.int32),
+            pltpu.SMEM(history_len.shape, jnp.int32),
             pltpu.VMEM((here, HD), bf),
             pltpu.VMEM((here, HD), bf),
             pltpu.VMEM((slots // BLOCK, BLOCK, HD), bf),
@@ -373,14 +375,14 @@
             pltpu.VMEM((ring, 2, 2, 1, rows), f32),
             pltpu.VMEM((len(MESSAGES), HD, rows), bf),
             pltpu.VMEM((len(MESSAGES), 1, rows), f32),
-            dma((heads + 4,)),
+            dma((heads + 6,)),
             dma((len(QUERIES),)),
             dma((ring, 2, 2)),
             dma((len(MESSAGES), 2)),
             dma((len(MESSAGES), 2)),
         ],
         compiler_params=pltpu.CompilerParams(
-            collective_id=0, has_side_effects=True, vmem_limit_bytes=52 * 2**20
+            collective_id=0, has_side_effects=True, vmem_limit_bytes=63 * 2**20
         ),
         cost_estimate=pl.CostEstimate(
             flops=4 * all_rows * keys * HD,

time: 57.8 us -> 54.4 us (0.941)
  local copies, waits for them, and re-layouts: 4.94 us -> 1.67 us
    unnamed x13 -> x1, local copies, waits for them, and re-layouts: 4.94 us -> 1.67 us
where the time goes in v3:
time: 54.4 us; the launch traced here: 54.3 us
  Pallas kernels  52.6 us (97%)
  local copies, waits for them, and re-layouts  1.67 us (3%)
    pallas_call x1, Pallas kernels, local(): pl.pallas_call(functools.partial(kernel, ring), out_shape=jax.ShapeDtypeS...  52.6 us
    unnamed x1, local copies, waits for them, and re-layouts  1.67 us

profile of v3, /device:TPU:16, one launch (start us, length us, event | category | flops | bytes accessed | tf_op | source)
XLA Modules:
  0.0 54.3 jit_solution(6227253983296365600)
XLA Ops:
  0.0 52.6 %shard_map.73 = f32[64,1024]{1,0:T(8,128)} custom-call(bf16[64,1024]{1,0:T(8,128)(2,1)} %q_in.1, bf16[64,128]{1,0:T(8,128)(2,1)} %nk_in.1, bf16[64,128]{1,0:T(8,128)(2,1)} %nv_in.1, bf16[16,256,128]{2,1,0:T(8,128)(2,1)} %bitcast.2, bf16[16,256,128]{2,1,0:T(8,128)(2,1)} %bitcast.3, s32[16]{0:T(128)} %owner_in.1, s32[2]{0:T(128)} %hist_in.1), custom_call_target="tpu_custom_call" | custom-call | flops 8858370048 | bytes 2490368 | tf_op jit(solution)/shard_map/pallas_call | solution.py:356
  52.6 1.7 %copy.9 = f32[64,1024]{1,0:T(8,128)} copy(f32[64,1024]{1,0:T(8,128)} %shard_map.73) | data formatting | bytes 524288

commit v4 on v3

--- a/solution.py
+++ b/solution.py
@@ -21,53 +21,53 @@
 
 ORDER = (
     (1, 0),
+    (0, 1),
     (7, 0),
-    (0, 1),
+    (7, 1),
     (2, 0),
-    (7, 1),
     (6, 0),
+    (6, 1),
     (3, 0),
     (5, 0),
-    (1, 1),
     (5, 1),
     (4, 0),
     (4, 1),
     (3, 1),
-    (6, 1),
+    (1, 1),
     (2, 1),
     (0, 0),
 )
 BEFORE = (
-    ((Q, 0, 0, 0, 1, 1), (Q, 0, 1, 0, 1, 0), (Q, 0, 0, 0, -1, 0), (Q, 0, 0, 0, 1, 0), (Q, 0, 0, 0, -1, 1), (Q, 0, 0, 0, 0, 1), (Q, 0, 1, 0, -1, 0), (Q, 0, 1, 0, 0, 1),),
-    (),
-    (),
-    (),
-    (),
-    (),
-    (),
-    (),
-    (),
-    ((Q, 1, 0, 0, -1, 0), (Q, 7, 0, 1, 1, 0), (Q, 7, 1, 0, 0, 1), (Q, 7, 1, 0, 1, 0), (Q, 1, 0, 1, -1, 0),),
-    ((Q, 7, 0, 0, 1, 0),),
+    ((Q, 0, 1, 0, 1, 0), (Q, 0, 0, 0, -1, 1), (Q, 0, 0, 0, -1, 0), (Q, 0, 1, 0, 0, 1), (Q, 0, 1, 0, -1, 0), (Q, 0, 0, 0, 1, 0), (Q, 0, 0, 0, 1, 1), (Q, 0, 0, 0, 0, 1),),
+    (),
+    (),
+    (),
+    (),
+    (),
+    (),
+    (),
+    (),
+    ((Q, 7, 1, 0, 0, 1), (Q, 7, 1, 0, 1, 0), (Q, 1, 0, 1, -1, 0), (Q, 7, 0, 0, 1, 0), (Q, 1, 0, 0, -1, 0),),
+    (),
 )
 AFTER = (
-    ((Q, 1, 1, 0, -1, 0), (Q, 2, 0, 0, -1, 0), (Q, 1, 1, 0, 0, 1),),
-    ((Q, 6, 1, 0, 1, 0), (Q, 6, 0, 1, 1, 0), (Q, 6, 1, 0, 0, 1), (Q, 2, 0, 1, -1, 0),),
-    ((Q, 6, 0, 0, 1, 0), (S, 0, 1, 1, 0, 1),),
-    ((Q, 2, 1, 0, -2, 0), (Q, 2, 1, 0, 0, 1), (Q, 2, 1, 0, -1, 0),),
-    ((Q, 5, 1, 0, 0, 1), (S, 7, 1, 1, 0, 1),),
-    ((Q, 5, 0, 1, 1, 0), (Q, 5, 0, 0, 1, 0),),
-    ((S, 3, 0, 1, 1, 0), (S, 3, 0, 0, 1, 0), (Q, 4, 1, 0, 0, 1),),
-    ((Q, 3, 1, 0, 0, 1), (S, 5, 0, 1, -1, 0), (S, 5, 0, 0, -1, 0),),
-    ((S, 1, 1, 1, 0, 1), (F, 7, 1, 0, ((7, 1, 1, 0, 1),)), (S, 7, 1, 0, -1, 0),),
-    ((F, 2, 0, 1, ((3, 0, 1, 1, 0),)), (S, 2, 0, 1, 1, 0), (S, 5, 1, 1, 0, 1),),
-    ((S, 4, 0, 1, -2, 0), (S, 4, 0, 0, 2, 0),),
-    ((S, 4, 1, 1, 0, 1), (F, 1, 1, 0, ((1, 1, 1, 0, 1),)), (S, 1, 1, 0, 1, 0), (F, 6, 0, 0, ((5, 0, 0, -1, 0),)), (S, 6, 0, 0, -1, 0),),
-    ((S, 3, 1, 1, 0, 1), (F, 5, 1, 0, ((5, 1, 1, 0, 1),)), (S, 5, 1, 0, -1, 0), (F, 1, 0, 1, ((2, 0, 1, 1, 0),)), (S, 1, 0, 1, 1, 1),),
-    ((F, 6, 0, 1, ((4, 0, 1, -2, 0), (5, 0, 1, -1, 0))), (S, 6, 0, 1, -1, 0), (F, 2, 0, 0, ((4, 0, 0, 2, 0), (3, 0, 0, 1, 0))), (S, 2, 0, 0, 1, 0), (S, 6, 1, 1, 0, 1), (F, 4, 1, 0, ((4, 1, 1, 0, 1),)), (S, 4, 1, 0, -2, 0),),
-    ((S, 2, 1, 1, 0, 1), (F, 7, 0, 0, ((6, 0, 0, -1, 0),)), (S, 7, 0, 0, -1, 0), (F, 3, 1, 0, ((3, 1, 1, 0, 1),)), (S, 3, 1, 0, 1, 0),),
-    ((S, 0, 0, 1, 0, 1),),
-    ((F, 7, 0, 1, ((6, 0, 1, -1, 0),)), (S, 7, 0, 1, -1, 1), (F, 6, 1, 0, ((6, 1, 1, 0, 1),)), (F, 1, 0, 0, ((2, 0, 0, 1, 0),)), (S, 1, 0, 0, 1, 0), (F, 6, 1, 0, ((4, 1, 0, -2, 0), (5, 1, 0, -1, 0))), (S, 6, 1, 0, -2, 0), (F, 2, 1, 0, ((2, 1, 1, 0, 1),)), (F, 2, 1, 0, ((3, 1, 0, 1, 0),)), (S, 2, 1, 0, 2, 0),),
+    ((Q, 7, 0, 1, 1, 0), (Q, 1, 1, 0, 0, 1), (Q, 1, 1, 0, -1, 0),),
+    ((Q, 6, 1, 0, 0, 1), (Q, 2, 0, 1, -1, 0), (Q, 6, 1, 0, 1, 0), (S, 0, 1, 1, 0, 1), (Q, 6, 0, 0, 1, 0),),
+    ((Q, 2, 0, 0, -1, 0),),
+    ((Q, 2, 1, 0, 0, 1), (Q, 6, 0, 1, 1, 0), (Q, 2, 1, 0, -1, 0), (S, 7, 1, 1, 0, 1),),
+    ((Q, 3, 0, 1, -1, 0), (Q, 5, 1, 0, 0, 1), (Q, 5, 1, 0, 1, 0), (Q, 5, 1, 0, 1, 1),),
+    ((Q, 3, 0, 0, -1, 0),),
+    ((Q, 3, 1, 0, 0, 1), (S, 6, 1, 1, 0, 1),),
+    ((S, 3, 0, 0, 1, 0), (S, 3, 0, 1, 1, 0), (F, 7, 1, 0, ((7, 1, 1, 0, 1),)), (S, 7, 1, 0, -1, 0),),
+    ((S, 5, 0, 0, -1, 0), (S, 5, 0, 1, -1, 0),),
+    ((S, 5, 1, 1, 0, 1),),
+    ((S, 4, 0, 0, 2, 0), (S, 4, 0, 1, -2, 0), (F, 6, 1, 0, ((6, 1, 1, 0, 1),)),),
+    ((F, 2, 0, 1, ((3, 0, 1, 1, 0),)), (S, 2, 0, 1, 1, 0), (S, 4, 1, 1, 0, 1), (F, 6, 0, 0, ((5, 0, 0, -1, 0),)), (S, 6, 0, 0, -1, 0),),
+    ((F, 5, 1, 0, ((5, 1, 1, 0, 1),)), (S, 5, 1, 0, -1, 0), (S, 3, 1, 1, 0, 1),),
+    ((F, 6, 0, 1, ((4, 0, 1, -2, 0), (5, 0, 1, -1, 0))), (S, 6, 0, 1, -1, 0), (F, 2, 0, 0, ((4, 0, 0, 2, 0), (3, 0, 0, 1, 0))), (S, 2, 0, 0, 1, 0), (S, 1, 1, 1, 0, 1),),
+    ((F, 4, 1, 0, ((4, 1, 1, 0, 1),)), (F, 1, 0, 1, ((2, 0, 1, 1, 0),)), (S, 1, 0, 1, 1, 1), (S, 4, 1, 0, -2, 0), (S, 2, 1, 1, 0, 1), (F, 7, 0, 0, ((6, 0, 0, -1, 0),)), (S, 7, 0, 0, -1, 0),),
+    ((F, 3, 1, 0, ((3, 1, 1, 0, 1),)), (S, 3, 1, 0, 1, 0), (S, 0, 0, 1, 0, 1),),
+    ((F, 1, 0, 0, ((2, 0, 0, 1, 0),)), (S, 1, 0, 0, 1, 0), (F, 1, 1, 0, ((1, 1, 1, 0, 1),)), (S, 1, 1, 0, 1, 0), (F, 7, 0, 1, ((6, 0, 1, -1, 0),)), (S, 7, 0, 1, -1, 1), (F, 6, 1, 0, ((4, 1, 0, -2, 0), (5, 1, 0, -1, 0))), (S, 6, 1, 0, -2, 0), (F, 2, 1, 0, ((2, 1, 1, 0, 1),)), (F, 2, 1, 0, ((3, 1, 0, 1, 0),)), (S, 2, 1, 0, 2, 0),),
 )
 LAST = (
     ((1, 0, 0, 1, 0), (7, 0, 0, -1, 0), (1, 0, 1, 1, 1), (7, 0, 1, -1, 1), (0, 0, 1, 0, 1),),
@@ -355,7 +355,7 @@
     keys = hist_rows + here
     return pl.pallas_call(
         functools.partial(kernel, ring),
-        out_shape=jax.ShapeDtypeStruct((here, width), f32),
+        out_shape=pltpu.VMEM((here, width), f32),
         in_specs=[hbm] * 7,
         out_specs=pl.BlockSpec(memory_space=pltpu.VMEM),
         scratch_shapes=[
@@ -382,7 +382,7 @@
             dma((len(MESSAGES), 2)),
         ],
         compiler_params=pltpu.CompilerParams(
-            collective_id=0, has_side_effects=True, vmem_limit_bytes=63 * 2**20
+            collective_id=0, has_side_effects=True, vmem_limit_bytes=54 * 2**20 - 0 * 2**10
         ),
         cost_estimate=pl.CostEstimate(
             flops=4 * all_rows * keys * HD,

time: 54.4 us -> 53 us (0.974)
  local copies, waits for them, and re-layouts: 1.67 us -> 0.71 us
    unnamed x1, local copies, waits for them, and re-layouts: 1.67 us -> 0.71 us
where the time goes in v4:
time: 53 us; the launch traced here: 52.9 us
  Pallas kernels  52.2 us (98%)
  local copies, waits for them, and re-layouts  0.71 us (1%)
    pallas_call x1, Pallas kernels, local(): pl.pallas_call(functools.partial(kernel, ring), out_shape=pltpu.VMEM((her...  52.2 us

profile of v4, /device:TPU:16, one launch (start us, length us, event | category | flops | bytes accessed | tf_op | source)
XLA Modules:
  0.0 52.9 jit_solution(6050350990199001874)
XLA Ops:
  0.0 52.2 %shard_map.73 = f32[64,1024]{1,0:T(8,128)S(1)} custom-call(bf16[64,1024]{1,0:T(8,128)(2,1)} %q_in.1, bf16[64,128]{1,0:T(8,128)(2,1)} %nk_in.1, bf16[64,128]{1,0:T(8,128)(2,1)} %nv_in.1, bf16[16,256,128]{2,1,0:T(8,128)(2,1)} %bitcast.2, bf16[16,256,128]{2,1,0:T(8,128)(2,1)} %bitcast.3, s32[16]{0:T(128)} %owner_in.1, s32[2]{0:T(128)} %hist_in.1), custom_call_target="tpu_custom_call" | custom-call | flops 8858370048 | bytes 2490368 | tf_op jit(solution)/shard_map/pallas_call | solution.py:356
  52.2 0.7 %copy.9 = f32[64,1024]{1,0:T(8,128)} copy(f32[64,1024]{1,0:T(8,128)S(1)} %shard_map.73) | data formatting | bytes 524288

commit v5 on v4

--- a/solution.py
+++ b/solution.py
@@ -26,48 +26,48 @@
     (7, 1),
     (2, 0),
     (6, 0),
-    (6, 1),
+    (1, 1),
     (3, 0),
     (5, 0),
     (5, 1),
     (4, 0),
     (4, 1),
     (3, 1),
-    (1, 1),
     (2, 1),
+    (6, 1),
     (0, 0),
 )
 BEFORE = (
-    ((Q, 0, 1, 0, 1, 0), (Q, 0, 0, 0, -1, 1), (Q, 0, 0, 0, -1, 0), (Q, 0, 1, 0, 0, 1), (Q, 0, 1, 0, -1, 0), (Q, 0, 0, 0, 1, 0), (Q, 0, 0, 0, 1, 1), (Q, 0, 0, 0, 0, 1),),
-    (),
-    (),
-    (),
-    (),
-    (),
-    (),
-    (),
-    (),
-    ((Q, 7, 1, 0, 0, 1), (Q, 7, 1, 0, 1, 0), (Q, 1, 0, 1, -1, 0), (Q, 7, 0, 0, 1, 0), (Q, 1, 0, 0, -1, 0),),
+    ((Q, 0, 0, 0, -1, 1), (Q, 0, 1, 0, 1, 0), (Q, 0, 0, 0, 1, 0), (Q, 0, 1, 0, 0, 1), (Q, 0, 0, 0, -1, 0), (Q, 0, 0, 0, 1, 1), (Q, 0, 1, 0, -1, 0), (Q, 0, 0, 0, 0, 1),),
+    (),
+    (),
+    (),
+    (),
+    (),
+    (),
+    (),
+    (),
+    ((Q, 7, 1, 0, 1, 0), (Q, 7, 1, 0, 0, 1), (Q, 1, 0, 1, -1, 0), (Q, 1, 0, 0, -1, 0), (Q, 7, 0, 0, 1, 0),),
     (),
 )
 AFTER = (
-    ((Q, 7, 0, 1, 1, 0), (Q, 1, 1, 0, 0, 1), (Q, 1, 1, 0, -1, 0),),
-    ((Q, 6, 1, 0, 0, 1), (Q, 2, 0, 1, -1, 0), (Q, 6, 1, 0, 1, 0), (S, 0, 1, 1, 0, 1), (Q, 6, 0, 0, 1, 0),),
-    ((Q, 2, 0, 0, -1, 0),),
-    ((Q, 2, 1, 0, 0, 1), (Q, 6, 0, 1, 1, 0), (Q, 2, 1, 0, -1, 0), (S, 7, 1, 1, 0, 1),),
-    ((Q, 3, 0, 1, -1, 0), (Q, 5, 1, 0, 0, 1), (Q, 5, 1, 0, 1, 0), (Q, 5, 1, 0, 1, 1),),
-    ((Q, 3, 0, 0, -1, 0),),
-    ((Q, 3, 1, 0, 0, 1), (S, 6, 1, 1, 0, 1),),
-    ((S, 3, 0, 0, 1, 0), (S, 3, 0, 1, 1, 0), (F, 7, 1, 0, ((7, 1, 1, 0, 1),)), (S, 7, 1, 0, -1, 0),),
+    ((Q, 1, 1, 0, -1, 0), (Q, 1, 1, 0, 0, 1), (Q, 7, 0, 1, 1, 0),),
+    ((Q, 6, 1, 0, 0, 1), (Q, 2, 0, 1, -1, 0), (Q, 6, 1, 0, 1, 0), (S, 0, 1, 1, 0, 1),),
+    ((Q, 6, 0, 0, 1, 0), (Q, 2, 0, 0, -1, 0),),
+    ((Q, 2, 1, 0, -2, 0), (Q, 2, 1, 0, 0, 1), (Q, 6, 0, 1, 1, 0), (Q, 2, 1, 0, -1, 0), (S, 7, 1, 1, 0, 1),),
+    ((Q, 3, 0, 1, -1, 0), (Q, 5, 1, 0, 0, 1),),
+    ((Q, 5, 0, 0, 1, 0),),
+    ((Q, 4, 1, 0, 0, 1), (S, 1, 1, 1, 0, 1),),
+    ((F, 7, 1, 0, ((7, 1, 1, 0, 1),)), (S, 7, 1, 0, -1, 0), (S, 3, 0, 0, 1, 0), (S, 3, 0, 1, 1, 0), (Q, 3, 1, 0, 0, 1),),
     ((S, 5, 0, 0, -1, 0), (S, 5, 0, 1, -1, 0),),
     ((S, 5, 1, 1, 0, 1),),
-    ((S, 4, 0, 0, 2, 0), (S, 4, 0, 1, -2, 0), (F, 6, 1, 0, ((6, 1, 1, 0, 1),)),),
-    ((F, 2, 0, 1, ((3, 0, 1, 1, 0),)), (S, 2, 0, 1, 1, 0), (S, 4, 1, 1, 0, 1), (F, 6, 0, 0, ((5, 0, 0, -1, 0),)), (S, 6, 0, 0, -1, 0),),
-    ((F, 5, 1, 0, ((5, 1, 1, 0, 1),)), (S, 5, 1, 0, -1, 0), (S, 3, 1, 1, 0, 1),),
-    ((F, 6, 0, 1, ((4, 0, 1, -2, 0), (5, 0, 1, -1, 0))), (S, 6, 0, 1, -1, 0), (F, 2, 0, 0, ((4, 0, 0, 2, 0), (3, 0, 0, 1, 0))), (S, 2, 0, 0, 1, 0), (S, 1, 1, 1, 0, 1),),
-    ((F, 4, 1, 0, ((4, 1, 1, 0, 1),)), (F, 1, 0, 1, ((2, 0, 1, 1, 0),)), (S, 1, 0, 1, 1, 1), (S, 4, 1, 0, -2, 0), (S, 2, 1, 1, 0, 1), (F, 7, 0, 0, ((6, 0, 0, -1, 0),)), (S, 7, 0, 0, -1, 0),),
-    ((F, 3, 1, 0, ((3, 1, 1, 0, 1),)), (S, 3, 1, 0, 1, 0), (S, 0, 0, 1, 0, 1),),
-    ((F, 1, 0, 0, ((2, 0, 0, 1, 0),)), (S, 1, 0, 0, 1, 0), (F, 1, 1, 0, ((1, 1, 1, 0, 1),)), (S, 1, 1, 0, 1, 0), (F, 7, 0, 1, ((6, 0, 1, -1, 0),)), (S, 7, 0, 1, -1, 1), (F, 6, 1, 0, ((4, 1, 0, -2, 0), (5, 1, 0, -1, 0))), (S, 6, 1, 0, -2, 0), (F, 2, 1, 0, ((2, 1, 1, 0, 1),)), (F, 2, 1, 0, ((3, 1, 0, 1, 0),)), (S, 2, 1, 0, 2, 0),),
+    ((S, 4, 0, 1, -2, 0), (S, 4, 0, 0, 2, 0), (F, 1, 1, 0, ((1, 1, 1, 0, 1),)), (S, 1, 1, 0, 1, 0),),
+    ((F, 6, 0, 0, ((5, 0, 0, -1, 0),)), (S, 6, 0, 0, -1, 0), (F, 2, 0, 1, ((3, 0, 1, 1, 0),)), (S, 2, 0, 1, 1, 0), (S, 4, 1, 1, 0, 1),),
+    ((S, 3, 1, 1, 0, 1), (F, 5, 1, 0, ((5, 1, 1, 0, 1),)), (S, 5, 1, 0, -1, 0),),
+    ((F, 2, 0, 0, ((4, 0, 0, 2, 0), (3, 0, 0, 1, 0))), (S, 2, 0, 0, 1, 0), (S, 2, 1, 1, 0, 1), (F, 6, 0, 1, ((4, 0, 1, -2, 0), (5, 0, 1, -1, 0))), (S, 6, 0, 1, -1, 0),),
+    ((S, 6, 1, 1, 0, 1), (F, 4, 1, 0, ((4, 1, 1, 0, 1),)), (S, 4, 1, 0, -2, 0), (F, 7, 0, 0, ((6, 0, 0, -1, 0),)), (S, 7, 0, 0, -1, 0),),
+    ((F, 3, 1, 0, ((3, 1, 1, 0, 1),)), (S, 3, 1, 0, 1, 0), (S, 0, 0, 1, 0, 1), (F, 1, 0, 1, ((2, 0, 1, 1, 0),)), (S, 1, 0, 1, 1, 1),),
+    ((F, 2, 1, 0, ((2, 1, 1, 0, 1),)), (F, 7, 0, 1, ((6, 0, 1, -1, 0),)), (S, 7, 0, 1, -1, 1), (F, 1, 0, 0, ((2, 0, 0, 1, 0),)), (S, 1, 0, 0, 1, 0), (F, 6, 1, 0, ((6, 1, 1, 0, 1),)), (F, 6, 1, 0, ((4, 1, 0, -2, 0), (5, 1, 0, -1, 0))), (S, 6, 1, 0, -2, 0), (F, 2, 1, 0, ((3, 1, 0, 1, 0),)), (S, 2, 1, 0, 2, 0),),
 )
 LAST = (
     ((1, 0, 0, 1, 0), (7, 0, 0, -1, 0), (1, 0, 1, 1, 1), (7, 0, 1, -1, 1), (0, 0, 1, 0, 1),),
@@ -382,7 +382,7 @@
             dma((len(MESSAGES), 2)),
         ],
         compiler_params=pltpu.CompilerParams(
-            collective_id=0, has_side_effects=True, vmem_limit_bytes=54 * 2**20 - 0 * 2**10
+            collective_id=0, has_side_effects=True, vmem_limit_bytes=54 * 2**20
         ),
         cost_estimate=pl.CostEstimate(
             flops=4 * all_rows * keys * HD,

time: 53 us -> 52.8 us (level)
  no operation moved by 1% of the time
where the time goes in v5:
time: 52.8 us; the launch traced here: 52.7 us
  Pallas kernels  52 us (98%)
  local copies, waits for them, and re-layouts  0.71 us (1%)
    pallas_call x1, Pallas kernels, local(): pl.pallas_call(functools.partial(kernel, ring), out_shape=pltpu.VMEM((her...  52 us

profile of v5, /device:TPU:16, one launch (start us, length us, event | category | flops | bytes accessed | tf_op | source)
XLA Modules:
  0.0 52.7 jit_solution(12715711755431060588)
XLA Ops:
  0.0 52.0 %shard_map.73 = f32[64,1024]{1,0:T(8,128)S(1)} custom-call(bf16[64,1024]{1,0:T(8,128)(2,1)} %q_in.1, bf16[64,128]{1,0:T(8,128)(2,1)} %nk_in.1, bf16[64,128]{1,0:T(8,128)(2,1)} %nv_in.1, bf16[16,256,128]{2,1,0:T(8,128)(2,1)} %bitcast.2, bf16[16,256,128]{2,1,0:T(8,128)(2,1)} %bitcast.3, s32[16]{0:T(128)} %owner_in.1, s32[2]{0:T(128)} %hist_in.1), custom_call_target="tpu_custom_call" | custom-call | flops 8858370048 | bytes 2490368 | tf_op jit(solution)/shard_map/pallas_call | solution.py:356
  52.0 0.7 %copy.9 = f32[64,1024]{1,0:T(8,128)} copy(f32[64,1024]{1,0:T(8,128)S(1)} %shard_map.73) | data formatting | bytes 524288

commit v6 on v5

--- a/solution.py
+++ b/solution.py
@@ -332,13 +332,13 @@
     absorb(last, s1)
     for event in after[last] + after[last + 1]:
         act(event)
-    finish(A)
-    finish(B)
     for n in range(len(QUERIES)):
         q_copy(n).wait_send()
     for n in range(len(MESSAGES)):
         for copy in p_copies(n):
             copy.wait_send()
+    finish(A)
+    finish(B)
 
 
 def local(queries, new_keys, new_values, cache_keys, cache_values, block_owner, history_len):

time: 52.8 us -> 52.6 us (level)
  no operation moved by 1% of the time
where the time goes in v6:
time: 52.6 us; the launch traced here: 52.5 us
  Pallas kernels  51.8 us (98%)
  local copies, waits for them, and re-layouts  0.71 us (1%)
    pallas_call x1, Pallas kernels, local(): pl.pallas_call(functools.partial(kernel, ring), out_shape=pltpu.VMEM((her...  51.8 us

profile of v6, /device:TPU:16, one launch (start us, length us, event | category | flops | bytes accessed | tf_op | source)
XLA Modules:
  0.0 52.5 jit_solution(3081131313985340945)
XLA Ops:
  0.0 51.8 %shard_map.73 = f32[64,1024]{1,0:T(8,128)S(1)} custom-call(bf16[64,1024]{1,0:T(8,128)(2,1)} %q_in.1, bf16[64,128]{1,0:T(8,128)(2,1)} %nk_in.1, bf16[64,128]{1,0:T(8,128)(2,1)} %nv_in.1, bf16[16,256,128]{2,1,0:T(8,128)(2,1)} %bitcast.2, bf16[16,256,128]{2,1,0:T(8,128)(2,1)} %bitcast.3, s32[16]{0:T(128)} %owner_in.1, s32[2]{0:T(128)} %hist_in.1), custom_call_target="tpu_custom_call" | custom-call | flops 8858370048 | bytes 2490368 | tf_op jit(solution)/shard_map/pallas_call | solution.py:356
  51.8 0.7 %copy.9 = f32[64,1024]{1,0:T(8,128)} copy(f32[64,1024]{1,0:T(8,128)S(1)} %shard_map.73) | data formatting | bytes 524288

commit v7 on v6

--- a/solution.py
+++ b/solution.py
@@ -176,8 +176,8 @@
             acc = term if acc is None else acc + term
         return acc, peak + jnp.log(total) * LOG2E
 
-    def take(p, g, c, messages):
-        parts = [(po.at[p, g, c], ps.at[p, g, c])]
+    def take(p, g, c, messages, start=None):
+        parts = [start or (po.at[p, g, c], ps.at[p, g, c])]
         for message in messages:
             n = MESSAGES.index(message)
             for copy in p_copies(n):
@@ -186,7 +186,10 @@
         return merged(parts)
 
     def finish(g):
-        acc, _ = take(0, g, OWN, LAST[g])
+        late = [m for m in LAST[g] if abs(m[3]) > 1]
+        acc, lse = take(0, g, OWN, [m for m in LAST[g] if m not in late])
+        if late:
+            acc, _ = take(0, g, OWN, late, (acc, lse))
         for h in range(heads):
             out[:, pl.ds((g * heads + h) * HD, HD)] = acc[:, h * here : (h + 1) * here].T
 

time: 52.6 us -> 52.6 us (level)
  no operation moved by 1% of the time
where the time goes in v7:
time: 52.6 us; the launch traced here: 52.5 us
  Pallas kernels  51.8 us (98%)
  local copies, waits for them, and re-layouts  0.71 us (1%)
    pallas_call x1, Pallas kernels, local(): pl.pallas_call(functools.partial(kernel, ring), out_shape=pltpu.VMEM((her...  51.8 us

profile of v7, /device:TPU:16, one launch (start us, length us, event | category | flops | bytes accessed | tf_op | source)
XLA Modules:
  0.0 52.5 jit_solution(1294589740593062658)
XLA Ops:
  0.0 51.8 %shard_map.73 = f32[64,1024]{1,0:T(8,128)S(1)} custom-call(bf16[64,1024]{1,0:T(8,128)(2,1)} %q_in.1, bf16[64,128]{1,0:T(8,128)(2,1)} %nk_in.1, bf16[64,128]{1,0:T(8,128)(2,1)} %nv_in.1, bf16[16,256,128]{2,1,0:T(8,128)(2,1)} %bitcast.2, bf16[16,256,128]{2,1,0:T(8,128)(2,1)} %bitcast.3, s32[16]{0:T(128)} %owner_in.1, s32[2]{0:T(128)} %hist_in.1), custom_call_target="tpu_custom_call" | custom-call | flops 8858370048 | bytes 2490368 | tf_op jit(solution)/shard_map/pallas_call | solution.py:359
  51.8 0.7 %copy.9 = f32[64,1024]{1,0:T(8,128)} copy(f32[64,1024]{1,0:T(8,128)S(1)} %shard_map.73) | data formatting | bytes 524288

commit v8 on v6

--- a/solution.py
+++ b/solution.py
@@ -20,54 +20,54 @@
 Q, S, F = 0, 1, 2
 
 ORDER = (
+    (7, 0),
+    (0, 0),
     (1, 0),
-    (0, 1),
-    (7, 0),
+    (1, 1),
+    (6, 0),
+    (2, 0),
     (7, 1),
-    (2, 0),
-    (6, 0),
-    (1, 1),
+    (5, 0),
     (3, 0),
-    (5, 0),
-    (5, 1),
+    (3, 1),
     (4, 0),
     (4, 1),
-    (3, 1),
+    (5, 1),
+    (6, 1),
     (2, 1),
-    (6, 1),
-    (0, 0),
+    (0, 1),
 )
 BEFORE = (
-    ((Q, 0, 0, 0, -1, 1), (Q, 0, 1, 0, 1, 0), (Q, 0, 0, 0, 1, 0), (Q, 0, 1, 0, 0, 1), (Q, 0, 0, 0, -1, 0), (Q, 0, 0, 0, 1, 1), (Q, 0, 1, 0, -1, 0), (Q, 0, 0, 0, 0, 1),),
-    (),
-    (),
-    (),
-    (),
-    (),
-    (),
-    (),
-    (),
-    ((Q, 7, 1, 0, 1, 0), (Q, 7, 1, 0, 0, 1), (Q, 1, 0, 1, -1, 0), (Q, 1, 0, 0, -1, 0), (Q, 7, 0, 0, 1, 0),),
+    ((Q, 0, 0, 0, 1, 1), (Q, 0, 1, 0, -1, 0), (Q, 0, 0, 0, 1, 0), (Q, 0, 1, 0, 1, 0), (Q, 0, 0, 0, -1, 0), (Q, 0, 0, 0, 0, 1), (Q, 0, 0, 0, -1, 1), (Q, 0, 1, 0, 0, 1),),
+    (),
+    (),
+    (),
+    (),
+    (),
+    (),
+    (),
+    (),
+    ((Q, 1, 1, 0, 0, 1), (Q, 1, 1, 0, -1, 0), (Q, 7, 0, 1, 1, 0), (Q, 7, 0, 0, 1, 0), (Q, 1, 0, 0, -1, 0),),
     (),
 )
 AFTER = (
-    ((Q, 1, 1, 0, -1, 0), (Q, 1, 1, 0, 0, 1), (Q, 7, 0, 1, 1, 0),),
-    ((Q, 6, 1, 0, 0, 1), (Q, 2, 0, 1, -1, 0), (Q, 6, 1, 0, 1, 0), (S, 0, 1, 1, 0, 1),),
+    ((Q, 7, 1, 0, 1, 0), (Q, 1, 0, 1, -1, 0), (Q, 7, 1, 0, 0, 1),),
+    ((Q, 2, 1, 0, -1, 0), (Q, 6, 0, 1, 1, 0), (Q, 2, 1, 0, 0, 1), (S, 0, 0, 1, 0, 1),),
     ((Q, 6, 0, 0, 1, 0), (Q, 2, 0, 0, -1, 0),),
-    ((Q, 2, 1, 0, -2, 0), (Q, 2, 1, 0, 0, 1), (Q, 6, 0, 1, 1, 0), (Q, 2, 1, 0, -1, 0), (S, 7, 1, 1, 0, 1),),
-    ((Q, 3, 0, 1, -1, 0), (Q, 5, 1, 0, 0, 1),),
+    ((Q, 6, 1, 0, 0, 1), (Q, 2, 0, 1, -1, 0), (Q, 6, 1, 0, 1, 0), (S, 1, 1, 1, 0, 1),),
+    ((Q, 3, 1, 0, 0, 1), (Q, 5, 0, 1, 1, 0), (Q, 3, 1, 0, -1, 1), (Q, 3, 1, 0, -1, 0),),
     ((Q, 5, 0, 0, 1, 0),),
-    ((Q, 4, 1, 0, 0, 1), (S, 1, 1, 1, 0, 1),),
-    ((F, 7, 1, 0, ((7, 1, 1, 0, 1),)), (S, 7, 1, 0, -1, 0), (S, 3, 0, 0, 1, 0), (S, 3, 0, 1, 1, 0), (Q, 3, 1, 0, 0, 1),),
-    ((S, 5, 0, 0, -1, 0), (S, 5, 0, 1, -1, 0),),
-    ((S, 5, 1, 1, 0, 1),),
-    ((S, 4, 0, 1, -2, 0), (S, 4, 0, 0, 2, 0), (F, 1, 1, 0, ((1, 1, 1, 0, 1),)), (S, 1, 1, 0, 1, 0),),
-    ((F, 6, 0, 0, ((5, 0, 0, -1, 0),)), (S, 6, 0, 0, -1, 0), (F, 2, 0, 1, ((3, 0, 1, 1, 0),)), (S, 2, 0, 1, 1, 0), (S, 4, 1, 1, 0, 1),),
-    ((S, 3, 1, 1, 0, 1), (F, 5, 1, 0, ((5, 1, 1, 0, 1),)), (S, 5, 1, 0, -1, 0),),
-    ((F, 2, 0, 0, ((4, 0, 0, 2, 0), (3, 0, 0, 1, 0))), (S, 2, 0, 0, 1, 0), (S, 2, 1, 1, 0, 1), (F, 6, 0, 1, ((4, 0, 1, -2, 0), (5, 0, 1, -1, 0))), (S, 6, 0, 1, -1, 0),),
-    ((S, 6, 1, 1, 0, 1), (F, 4, 1, 0, ((4, 1, 1, 0, 1),)), (S, 4, 1, 0, -2, 0), (F, 7, 0, 0, ((6, 0, 0, -1, 0),)), (S, 7, 0, 0, -1, 0),),
-    ((F, 3, 1, 0, ((3, 1, 1, 0, 1),)), (S, 3, 1, 0, 1, 0), (S, 0, 0, 1, 0, 1), (F, 1, 0, 1, ((2, 0, 1, 1, 0),)), (S, 1, 0, 1, 1, 1),),
-    ((F, 2, 1, 0, ((2, 1, 1, 0, 1),)), (F, 7, 0, 1, ((6, 0, 1, -1, 0),)), (S, 7, 0, 1, -1, 1), (F, 1, 0, 0, ((2, 0, 0, 1, 0),)), (S, 1, 0, 0, 1, 0), (F, 6, 1, 0, ((6, 1, 1, 0, 1),)), (F, 6, 1, 0, ((4, 1, 0, -2, 0), (5, 1, 0, -1, 0))), (S, 6, 1, 0, -2, 0), (F, 2, 1, 0, ((3, 1, 0, 1, 0),)), (S, 2, 1, 0, 2, 0),),
+    ((Q, 5, 1, 0, 0, 1), (S, 7, 1, 1, 0, 1),),
+    ((S, 5, 0, 0, -1, 0), (S, 5, 0, 1, -1, 0), (F, 1, 1, 0, ((1, 1, 1, 0, 1),)), (S, 1, 1, 0, 1, 0),),
+    ((S, 3, 0, 0, 1, 0), (S, 3, 0, 1, 1, 0),),
+    ((S, 3, 1, 1, 0, 1),),
+    ((S, 4, 0, 1, 2, 0), (S, 4, 0, 0, -2, 0), (F, 7, 1, 0, ((7, 1, 1, 0, 1),)), (S, 7, 1, 0, -1, 0),),
+    ((S, 4, 1, 1, 0, 1), (F, 2, 0, 0, ((3, 0, 0, 1, 0),)), (S, 2, 0, 0, 1, 0), (F, 6, 0, 1, ((5, 0, 1, -1, 0),)), (S, 6, 0, 1, -1, 0),),
+    ((S, 5, 1, 1, 0, 1), (F, 3, 1, 0, ((3, 1, 1, 0, 1),)), (S, 3, 1, 0, 1, 0),),
+    ((F, 6, 0, 0, ((4, 0, 0, -2, 0), (5, 0, 0, -1, 0))), (S, 6, 0, 0, -1, 0), (S, 6, 1, 1, 0, 1), (F, 2, 0, 1, ((4, 0, 1, 2, 0), (3, 0, 1, 1, 0))), (S, 2, 0, 1, 1, 0),),
+    ((F, 4, 1, 0, ((4, 1, 1, 0, 1),)), (S, 4, 1, 0, 2, 0), (S, 2, 1, 1, 0, 1), (F, 1, 0, 0, ((2, 0, 0, 1, 0),)), (S, 1, 0, 0, 1, 0),),
+    ((F, 5, 1, 0, ((5, 1, 1, 0, 1),)), (S, 5, 1, 0, -1, 0), (S, 0, 1, 1, 0, 1), (F, 7, 0, 1, ((6, 0, 1, -1, 0),)), (S, 7, 0, 1, -1, 1),),
+    ((F, 6, 1, 0, ((6, 1, 1, 0, 1),)), (F, 1, 0, 1, ((2, 0, 1, 1, 0),)), (S, 1, 0, 1, 1, 1), (F, 7, 0, 0, ((6, 0, 0, -1, 0),)), (S, 7, 0, 0, -1, 0), (F, 2, 1, 0, ((2, 1, 1, 0, 1),)), (F, 2, 1, 0, ((4, 1, 0, 2, 0), (3, 1, 0, 1, 0))), (S, 2, 1, 0, 2, 0), (F, 6, 1, 0, ((5, 1, 0, -1, 0),)), (S, 6, 1, 0, -2, 0),),
 )
 LAST = (
     ((1, 0, 0, 1, 0), (7, 0, 0, -1, 0), (1, 0, 1, 1, 1), (7, 0, 1, -1, 1), (0, 0, 1, 0, 1),),

time: 52.6 us -> 52.6 us (level)
  no operation moved by 1% of the time
where the time goes in v8:
time: 52.6 us; the launch traced here: 52.5 us
  Pallas kernels  51.8 us (98%)
  local copies, waits for them, and re-layouts  0.71 us (1%)
    pallas_call x1, Pallas kernels, local(): pl.pallas_call(functools.partial(kernel, ring), out_shape=pltpu.VMEM((her...  51.8 us

profile of v8, /device:TPU:16, one launch (start us, length us, event | category | flops | bytes accessed | tf_op | source)
XLA Modules:
  0.0 52.5 jit_solution(4829358730132465547)
XLA Ops:
  0.0 51.8 %shard_map.73 = f32[64,1024]{1,0:T(8,128)S(1)} custom-call(bf16[64,1024]{1,0:T(8,128)(2,1)} %q_in.1, bf16[64,128]{1,0:T(8,128)(2,1)} %nk_in.1, bf16[64,128]{1,0:T(8,128)(2,1)} %nv_in.1, bf16[16,256,128]{2,1,0:T(8,128)(2,1)} %bitcast.2, bf16[16,256,128]{2,1,0:T(8,128)(2,1)} %bitcast.3, s32[16]{0:T(128)} %owner_in.1, s32[2]{0:T(128)} %hist_in.1), custom_call_target="tpu_custom_call" | custom-call | flops 8858370048 | bytes 2490368 | tf_op jit(solution)/shard_map/pallas_call | solution.py:356
  51.8 0.7 %copy.9 = f32[64,1024]{1,0:T(8,128)} copy(f32[64,1024]{1,0:T(8,128)S(1)} %shard_map.73) | data formatting | bytes 524288
